TPU v7x, 32 devices: a whole 2x2x4 slice. The times are simulated.
32 devices in a mesh: dp: 4 (over z), grp: 2 (over y), wid: 4 (over x, core).
Axes of the slice: x: 2, y: 2, z: 4, core: 2. Of those that a mesh axis runs over, the one named last changes fastest.
Arguments:
- hidden_in: bfloat16 [4, 1024, 896], P('dp', None, 'wid'), may hold values from -26 to 26
- doc_ids: int32 [4, 1024], P('dp'), may hold values from 0 to 4, as said below
- qkv_weight: bfloat16 [2, 896, 1152], P(None, 'wid', 'grp'), may hold values from -0.1875 to 0.1875
- qkv_bias: float32 [2, 1152], P(None, 'grp'), may hold values from -3 to 3
- out_weight: bfloat16 [2, 896, 896], P(None, 'grp', 'wid'), may hold values from -1 to 1
- gate_up: bfloat16 [2, 896, 2, 4864], P(None, 'wid', None, 'grp'), may hold values from -0.1875 to 0.1875
- down_weight: bfloat16 [2, 4864, 896], P(None, 'grp', 'wid'), may hold values from -0.078125 to 0.078125
- norm_gains: float32 [2, 2, 896], P(None, None, 'wid'), may hold values from 0.25 to 1.75
- cotangent: bfloat16 [4, 1024, 896], P('dp', None, 'wid'), may hold values from -6 to 6
Outputs:
- hidden_out: bfloat16 [4, 1024, 896], P('dp', None, 'wid')
- input_grad: float32 [4, 1024, 896], P('dp', None, 'wid')
- qkv_weight_grad: float32 [2, 896, 1152], P(None, ('wid', 'dp'), 'grp')
- qkv_bias_grad: float32 [2, 1152], P(None, ('grp', 'dp'))
- out_weight_grad: float32 [2, 896, 896], P(None, ('grp', 'dp'), 'wid')
- gate_up_grad: float32 [2, 896, 2, 4864], P(None, ('wid', 'dp'), None, 'grp')
- down_weight_grad: float32 [2, 4864, 896], P(None, ('grp', 'dp'), 'wid')
- norm_gains_grad: float32 [2, 2, 896], P(None, None, ('wid', 'dp'))
Inputs may be any that keep to these rules, and one draw needn't show every extreme that they name: `doc_ids`: document numbers start at 0 in each sequence and never fall along it; every sequence holds five documents.
All inputs are finite; a program needn't handle non-finite values.
Results may differ from a plain program's by a relative error of at most 0.039.
Values may be sent and summed in bfloat16 or wider, within the bound.
A program may use at most 192 MiB of HBM per device.

v0:
```python
import jax
import jax.numpy as jnp
from jax import lax
from jax.sharding import PartitionSpec as P

D = 896
HEADS = 14
KV_HEADS = 2
HEAD_DIM = 64
LAYERS = 2


EPSILON = 1e-06
ROPE_BASE = 1000000.0
NEGATIVE = -1e30


def rope_tables(doc_ids, offset, span_rows):
    position_grid = lax.broadcasted_iota(jnp.int32, doc_ids.shape, 1)
    change = jnp.concatenate(
        [jnp.ones_like(doc_ids[:, :1]), (doc_ids[:, 1:] != doc_ids[:, :-1]).astype(jnp.int32)],
        axis=1,
    )
    starts = lax.cummax(jnp.where(change > 0, position_grid, 0), axis=1)
    places = (position_grid - starts).astype(jnp.float32)
    places = jnp.transpose(lax.dynamic_slice_in_dim(places, offset, span_rows, 1))
    frequency = ROPE_BASE ** (-jnp.arange(HEAD_DIM // 2, dtype=jnp.float32) / (HEAD_DIM // 2))
    angles = places[:, :, None] * frequency
    return (jnp.cos(angles), jnp.sin(angles))


def rotate(values, cosine_table, sine_table):
    half_width = values.shape[-1] // 2
    lower_half = values[..., :half_width]
    upper_half = values[..., half_width:]
    return jnp.concatenate(
        [
            lower_half * cosine_table - upper_half * sine_table,
            upper_half * cosine_table + lower_half * sine_table,
        ],
        axis=-1,
    )


def contract(left_side, weight, flipped):
    if flipped:
        return lax.dot_general(
            left_side, weight, (((1,), (1,)), ((), ())), preferred_element_type=jnp.float32
        )
    return jnp.dot(left_side, weight, preferred_element_type=jnp.float32)


def transposed_product(left_side, right_side):
    return lax.dot_general(
        left_side, right_side, (((0,), (0,)), ((), ())), preferred_element_type=jnp.float32
    )


def width_total(vector):
    return lax.psum(vector, "wid")


def head_total(partial_rows):
    return lax.psum(partial_rows.astype(jnp.bfloat16), "grp").astype(jnp.float32)


def gather_rows(values):
    return lax.all_gather(values, "wid", axis=0, tiled=True)


def row_products(values, weight, flipped):
    return lax.psum_scatter(
        contract(values, weight, flipped).astype(jnp.bfloat16),
        "wid",
        scatter_dimension=0,
        tiled=True,
    ).astype(jnp.float32)


def normalize(values, gain_row):
    scale_rows = lax.rsqrt(width_total(jnp.sum(values * values, axis=1)) / D + EPSILON)[:, None]
    return ((values * scale_rows * gain_row).astype(jnp.bfloat16), scale_rows)


def normalize_back(values, gain_row, scale_rows, grad_norm):
    inner_sum = width_total(jnp.sum(grad_norm * gain_row * values, axis=1))[:, None]
    grad_values = grad_norm * gain_row * scale_rows - values * scale_rows**3 * inner_sum / D
    grad_gain = jnp.sum(grad_norm * values * scale_rows, axis=0)
    return (grad_values, grad_gain)


def attend(queries, key_rows, value_rows, allowed):
    scores = jnp.einsum(
        "qsghd,ksgd->sghqk", queries, key_rows, preferred_element_type=jnp.float32
    ) * HEAD_DIM ** (-0.5)
    scores = jnp.where(allowed[:, None, None], scores, NEGATIVE)
    row_peak = jnp.max(scores, axis=-1, keepdims=True)
    raised = jnp.exp(scores - row_peak)
    row_total = jnp.sum(raised, axis=-1, keepdims=True)
    softened = (raised / row_total).astype(jnp.bfloat16)
    attended = jnp.einsum(
        "sghqk,ksgd->qsghd", softened, value_rows, preferred_element_type=jnp.float32
    )
    return (attended.astype(jnp.bfloat16), row_peak + jnp.log(row_total))


def attend_back(queries, key_rows, value_rows, allowed, logsum, grad_mix):
    scores = jnp.einsum(
        "qsghd,ksgd->sghqk", queries, key_rows, preferred_element_type=jnp.float32
    ) * HEAD_DIM ** (-0.5)
    scores = jnp.where(allowed[:, None, None], scores, NEGATIVE)
    softened = jnp.exp(scores - logsum)
    rounded = softened.astype(jnp.bfloat16)
    grad_soft = jnp.einsum(
        "qsghd,ksgd->sghqk", grad_mix, value_rows, preferred_element_type=jnp.float32
    )
    inner_sum = jnp.sum(softened * grad_soft, axis=-1, keepdims=True)
    grad_scores = (softened * (grad_soft - inner_sum)).astype(jnp.bfloat16)
    grad_query = jnp.einsum(
        "sghqk,ksgd->qsghd", grad_scores, key_rows, preferred_element_type=jnp.float32
    ) * HEAD_DIM ** (-0.5)
    grad_key = jnp.einsum(
        "sghqk,qsghd->ksgd", grad_scores, queries, preferred_element_type=jnp.float32
    ) * HEAD_DIM ** (-0.5)
    grad_value = jnp.einsum(
        "sghqk,qsghd->ksgd", rounded, grad_mix, preferred_element_type=jnp.float32
    )
    return (grad_query, grad_key, grad_value)


def layer_forward(residual, context, weights):
    cosine_table, sine_table, allowed = context
    qkv_w, qkv_b, out_w, gate_w, down_w, gain_rows = weights
    span_rows, seq_count = (cosine_table.shape[0], cosine_table.shape[1])
    heads_per = HEADS // KV_HEADS
    groups = qkv_w.shape[1] // ((heads_per + 2) * HEAD_DIM)
    normed, scale_one = normalize(residual, gain_rows[0])
    projected = (row_products(normed, qkv_w, False) + qkv_b).reshape(
        span_rows, seq_count, groups, heads_per + 2, HEAD_DIM
    )
    queries = rotate(
        projected[:, :, :, :heads_per], cosine_table[:, :, None, None], sine_table[:, :, None, None]
    ).astype(jnp.bfloat16)
    key_rot = rotate(
        projected[:, :, :, heads_per], cosine_table[:, :, None], sine_table[:, :, None]
    )
    key_value = jnp.stack([key_rot, projected[:, :, :, heads_per + 1]], axis=3).astype(jnp.bfloat16)
    key_value = lax.all_gather(
        key_value.reshape(span_rows * seq_count, -1), "wid", axis=0, tiled=True
    ).reshape(-1, seq_count, groups, 2, HEAD_DIM)
    attended, logsum = attend(queries, key_value[:, :, :, 0], key_value[:, :, :, 1], allowed)
    gathered_mix = gather_rows(attended.reshape(span_rows * seq_count, -1))
    after_attn = residual + head_total(
        jnp.dot(gathered_mix, out_w, preferred_element_type=jnp.float32)
    )
    normed_two, scale_two = normalize(after_attn, gain_rows[1])
    gate_both = row_products(normed_two, gate_w, False)
    width_ff = gate_both.shape[1] // 2
    product = (jax.nn.silu(gate_both[:, :width_ff]) * gate_both[:, width_ff:]).astype(jnp.bfloat16)
    gathered_hid = gather_rows(product)
    result = after_attn + head_total(
        jnp.dot(gathered_hid, down_w, preferred_element_type=jnp.float32)
    )
    stored = (
        residual,
        normed,
        scale_one,
        queries,
        key_value,
        logsum,
        gathered_mix,
        after_attn,
        normed_two,
        scale_two,
        gate_both,
        gathered_hid,
    )
    return (result, stored)


def layer_backward(gradient, stored, context, weights):
    cosine_table, sine_table, allowed = context
    qkv_w, qkv_b, out_w, gate_w, down_w, gain_rows = weights
    (
        residual,
        normed,
        scale_one,
        queries,
        key_value,
        logsum,
        gathered_mix,
        after_attn,
        normed_two,
        scale_two,
        gate_both,
        gathered_hid,
    ) = stored
    span_rows, seq_count = (cosine_table.shape[0], cosine_table.shape[1])
    grad_low = gradient.astype(jnp.bfloat16)
    grad_down = transposed_product(gathered_hid, grad_low)
    grad_hid = row_products(grad_low, down_w, True)
    width_ff = gate_both.shape[1] // 2
    gate_val = gate_both[:, :width_ff]
    up_val = gate_both[:, width_ff:]
    sigmoid_gate = jax.nn.sigmoid(gate_val)
    grad_gate = grad_hid * up_val * sigmoid_gate * (1.0 + gate_val * (1.0 - sigmoid_gate))
    grad_up = grad_hid * jax.nn.silu(gate_val)
    grad_both = gather_rows(jnp.concatenate([grad_gate, grad_up], axis=1).astype(jnp.bfloat16))
    grad_gate_w = transposed_product(normed_two, grad_both)
    grad_norm_two = head_total(contract(grad_both, gate_w, True))
    grad_after, gain_two = normalize_back(after_attn, gain_rows[1], scale_two, grad_norm_two)
    grad_after = gradient + grad_after
    grad_low_two = grad_after.astype(jnp.bfloat16)
    grad_out_w = transposed_product(gathered_mix, grad_low_two)
    grad_mix = row_products(grad_low_two, out_w, True).astype(jnp.bfloat16).reshape(queries.shape)
    grad_query, grad_key, grad_value = attend_back(
        queries, key_value[:, :, :, 0], key_value[:, :, :, 1], allowed, logsum, grad_mix
    )
    key_part = jnp.stack([grad_key, grad_value], axis=3)
    key_part = (
        lax.psum_scatter(
            key_part.reshape(key_part.shape[0] * seq_count, -1).astype(jnp.bfloat16),
            "wid",
            scatter_dimension=0,
            tiled=True,
        )
        .astype(jnp.float32)
        .reshape(span_rows, seq_count, -1, 2, HEAD_DIM)
    )
    back_query = rotate(grad_query, cosine_table[:, :, None, None], -sine_table[:, :, None, None])
    back_key = rotate(key_part[:, :, :, 0], cosine_table[:, :, None], -sine_table[:, :, None])
    grad_proj = jnp.concatenate(
        [back_query, back_key[:, :, :, None], key_part[:, :, :, 1:2]], axis=3
    ).astype(jnp.bfloat16)
    grad_proj = gather_rows(grad_proj.reshape(span_rows * seq_count, -1))
    grad_bias = jnp.sum(grad_proj, axis=0, dtype=jnp.float32)
    grad_qkv_w = transposed_product(normed, grad_proj)
    grad_norm_one = head_total(contract(grad_proj, qkv_w, True))
    grad_before, gain_one = normalize_back(residual, gain_rows[0], scale_one, grad_norm_one)
    shares = (
        lax.psum_scatter(
            grad_qkv_w.astype(jnp.bfloat16), "dp", scatter_dimension=0, tiled=True
        ).astype(jnp.float32),
        lax.psum_scatter(
            grad_bias.astype(jnp.bfloat16), "dp", scatter_dimension=0, tiled=True
        ).astype(jnp.float32),
        lax.psum_scatter(
            grad_out_w.astype(jnp.bfloat16), "dp", scatter_dimension=0, tiled=True
        ).astype(jnp.float32),
        lax.psum_scatter(
            grad_gate_w.astype(jnp.bfloat16), "dp", scatter_dimension=0, tiled=True
        ).astype(jnp.float32),
        lax.psum_scatter(
            grad_down.astype(jnp.bfloat16), "dp", scatter_dimension=0, tiled=True
        ).astype(jnp.float32),
        lax.psum_scatter(
            gain_one.astype(jnp.bfloat16), "dp", scatter_dimension=0, tiled=True
        ).astype(jnp.float32),
        lax.psum_scatter(
            gain_two.astype(jnp.bfloat16), "dp", scatter_dimension=0, tiled=True
        ).astype(jnp.float32),
    )
    return (grad_after + grad_before, shares)


def per_device(
    hidden_in,
    doc_ids,
    qkv_weight,
    qkv_bias,
    out_weight,
    gate_up,
    down_weight,
    norm_gains,
    cotangent,
):
    seq_count, length, width_own = hidden_in.shape
    span_rows = length // lax.axis_size("wid")
    offset = lax.axis_index("wid") * span_rows
    cosine_table, sine_table = rope_tables(doc_ids, offset, span_rows)
    query_doc = lax.dynamic_slice_in_dim(doc_ids, offset, span_rows, 1)
    query_place = offset + lax.iota(jnp.int32, span_rows)
    key_place = lax.iota(jnp.int32, length)
    allowed = (key_place[None, None, :] <= query_place[None, :, None]) & (
        query_doc[:, :, None] == doc_ids[:, None, :]
    )
    context = (cosine_table, sine_table, allowed)

    def pick_layer(layer_index):
        return (
            qkv_weight[layer_index],
            qkv_bias[layer_index],
            out_weight[layer_index],
            gate_up[layer_index].reshape(width_own, -1),
            down_weight[layer_index],
            norm_gains[layer_index],
        )

    residual = (
        jnp.transpose(hidden_in, (1, 0, 2))
        .reshape(length * seq_count, width_own)
        .astype(jnp.float32)
    )
    stored_all = []
    for layer_index in range(LAYERS):
        residual, stored = layer_forward(residual, context, pick_layer(layer_index))
        stored_all.append(stored)
    hidden_out = jnp.transpose(residual.reshape(length, seq_count, width_own), (1, 0, 2)).astype(
        jnp.bfloat16
    )
    gradient = (
        jnp.transpose(cotangent, (1, 0, 2))
        .reshape(length * seq_count, width_own)
        .astype(jnp.float32)
    )
    shares_all = []
    for layer_index in reversed(range(LAYERS)):
        gradient, shares = layer_backward(
            gradient, stored_all[layer_index], context, pick_layer(layer_index)
        )
        shares_all.append(shares)
    shares_all = shares_all[::-1]
    input_grad = jnp.transpose(gradient.reshape(length, seq_count, width_own), (1, 0, 2))
    qkv_weight_grad = jnp.stack([member[0] for member in shares_all])
    qkv_bias_grad = jnp.stack([member[1] for member in shares_all])
    out_weight_grad = jnp.stack([member[2] for member in shares_all])
    gate_up_grad = jnp.stack(
        [member[3].reshape(member[3].shape[0], 2, -1) for member in shares_all]
    )
    down_weight_grad = jnp.stack([member[4] for member in shares_all])
    norm_gains_grad = jnp.stack([jnp.stack([member[5], member[6]]) for member in shares_all])
    return (
        hidden_out,
        input_grad,
        qkv_weight_grad,
        qkv_bias_grad,
        out_weight_grad,
        gate_up_grad,
        down_weight_grad,
        norm_gains_grad,
    )


def solution(mesh):
    placed = (
        P("dp", None, "wid"),
        P("dp", None),
        P(None, "wid", "grp"),
        P(None, "grp"),
        P(None, "grp", "wid"),
        P(None, "wid", None, "grp"),
        P(None, "grp", "wid"),
        P(None, None, "wid"),
        P("dp", None, "wid"),
    )
    return jax.shard_map(
        per_device,
        mesh=mesh,
        in_specs=placed,
        out_specs=(
            P("dp", None, "wid"),
            P("dp", None, "wid"),
            P(None, ("wid", "dp"), "grp"),
            P(None, ("grp", "dp")),
            P(None, ("grp", "dp"), "wid"),
            P(None, ("wid", "dp"), None, "grp"),
            P(None, ("grp", "dp"), "wid"),
            P(None, None, ("wid", "dp")),
        ),
        check_vma=False,
    )
```

profile of v0, /device:TPU:0, one launch (start us, length us, event | category | flops | bytes accessed | tf_op | source)
XLA Modules:
  0.0 1365.5 jit_solution(8781388788573969970)
XLA Ops:
  8.4 8.3 psum.112
  25.5 22.6 %reduce-scatter.27.cloned.1.call-done = bf16[256,576]{0,1:T(8,128)(2,1)} async-done(((bf16[1024,576]{0,1:T(8,128)(2,1)}), bf16[256,576]{0,1:T(8,128)(2,1)}) %reduce-scatter.27.cloned.1.call-update) | async-done | bytes 294928 | tf_op jit(solution)/shard_map/reduce_scatter | solution.py:72
  49.5 5.8 all_gather.30
  61.0 9.4 all_gather.31
  72.7 5.8 fusion.194
  78.8 21.2 %all-reduce.18.cloned.1.call-done = bf16[1024,224]{0,1:T(8,128)(2,1)} async-done(((bf16[1024,224]{0,1:T(8,128)(2,1)}), bf16[1024,224]{0,1:T(8,128)(2,1)}) %all-reduce.18.cloned.1.call-update) | async-done | bytes 458768 | tf_op jit(solution)/shard_map/psum | solution.py:64
  101.2 6.9 psum.114
  108.7 6.7 convolution_convert_fusion.1
  115.5 81.1 %reduce-scatter.29.cloned.1.call-done = bf16[256,4864]{1,0:T(8,128)(2,1)} async-done(((bf16[1024,4864]{1,0:T(8,128)(2,1)}), bf16[256,4864]{1,0:T(8,128)(2,1)}) %reduce-scatter.29.cloned.1.call-update) | async-done | bytes 2490384 | tf_op jit(solution)/shard_map/reduce_scatter | solution.py:72
  203.0 38.8 %all-gather.7.cloned.1.call-done = bf16[1024,2432]{1,0:T(8,128)(2,1)} async-done(((bf16[256,2432]{1,0:T(8,128)(2,1)}), bf16[1024,2432]{1,0:T(8,128)(2,1)}) %all-gather.7.cloned.1.call-update) | async-done | bytes 4980752 | tf_op jit(solution)/shard_map/all_gather | solution.py:68
  247.0 27.3 %all-reduce.20.cloned.1.call-done = bf16[1024,224]{0,1:T(8,128)(2,1)} async-done(((bf16[1024,224]{0,1:T(8,128)(2,1)}), bf16[1024,224]{0,1:T(8,128)(2,1)}) %all-reduce.20.cloned.1.call-update) | async-done | bytes 458768 | tf_op jit(solution)/shard_map/psum | solution.py:64
  275.6 6.9 psum.116
  284.8 24.9 %reduce-scatter.31.cloned.1.call-done = bf16[256,576]{0,1:T(8,128)(2,1)} async-done(((bf16[1024,576]{0,1:T(8,128)(2,1)}), bf16[256,576]{0,1:T(8,128)(2,1)}) %reduce-scatter.31.cloned.1.call-update) | async-done | bytes 294928 | tf_op jit(solution)/shard_map/reduce_scatter | solution.py:72
  311.2 5.8 all_gather.33
  322.6 9.4 all_gather.34
  336.6 24.1 %all-reduce.22.cloned.1.call-done = bf16[1024,224]{0,1:T(8,128)(2,1)} async-done(((bf16[1024,224]{0,1:T(8,128)(2,1)}), bf16[1024,224]{0,1:T(8,128)(2,1)}) %all-reduce.22.cloned.1.call-update) | async-done | bytes 458768 | tf_op jit(solution)/shard_map/psum | solution.py:64
  361.9 6.9 psum.118
  369.4 7.1 convolution_convert_fusion
  382.8 74.8 %reduce-scatter.33.cloned.1.call-done = bf16[256,4864]{1,0:T(8,128)(2,1)} async-done(((bf16[1024,4864]{1,0:T(8,128)(2,1)}), bf16[256,4864]{1,0:T(8,128)(2,1)}) %reduce-scatter.33.cloned.1.call-update) | async-done | bytes 2490384 | tf_op jit(solution)/shard_map/reduce_scatter | solution.py:72
  461.9 48.1 %reduce-scatter.35.cloned.1.call-done = bf16[256,2432]{1,0:T(8,128)(2,1)} async-done(((bf16[1024,2432]{1,0:T(8,128)(2,1)}), bf16[256,2432]{1,0:T(8,128)(2,1)}) %reduce-scatter.35.cloned.1.call-update) | async-done | bytes 1245200 | tf_op jit(solution)/shard_map/reduce_scatter | solution.py:72
  517.1 67.3 %all-gather.11.cloned.1.call-done = bf16[1024,4864]{1,0:T(8,128)(2,1)} async-done(((bf16[256,4864]{1,0:T(8,128)(2,1)}), bf16[1024,4864]{1,0:T(8,128)(2,1)}) %all-gather.11.cloned.1.call-update) | async-done | bytes 9961488 | tf_op jit(solution)/shard_map/all_gather | solution.py:68
  584.5 7.6 convolution_convert_fusion.13
  592.2 27.3 %all-reduce.24.cloned.1.call-done = bf16[1024,224]{0,1:T(8,128)(2,1)} async-done(((bf16[1024,224]{0,1:T(8,128)(2,1)}), bf16[1024,224]{0,1:T(8,128)(2,1)}) %all-reduce.24.cloned.1.call-update) | async-done | bytes 458768 | tf_op jit(solution)/shard_map/psum | solution.py:64
  621.8 7.6 psum.121
  635.6 21.9 %reduce-scatter.37.cloned.1.call-done = bf16[256,448]{0,1:T(8,128)(2,1)} async-done(((bf16[1024,448]{0,1:T(8,128)(2,1)}), bf16[256,448]{0,1:T(8,128)(2,1)}) %reduce-scatter.37.cloned.1.call-update) | async-done | bytes 229392 | tf_op jit(solution)/shard_map/reduce_scatter | solution.py:72
  678.5 16.5 %reduce-scatter.39.cloned.1.call-done = bf16[256,128]{0,1:T(8,128)(2,1)} async-done(((bf16[1024,128]{0,1:T(8,128)(2,1)}), bf16[256,128]{0,1:T(8,128)(2,1)}) %reduce-scatter.39.cloned.1.call-update) | async-done | bytes 65552 | tf_op jit(solution)/shard_map/reduce_scatter | solution.py:221
  697.7 17.7 %all-gather.13.cloned.1.call-done = bf16[1024,576]{0,1:T(8,128)(2,1)} async-done(((bf16[256,576]{0,1:T(8,128)(2,1)}), bf16[1024,576]{0,1:T(8,128)(2,1)}) %all-gather.13.cloned.1.call-update) | async-done | bytes 1179664 | tf_op jit(solution)/shard_map/all_gather | solution.py:68
  718.0 27.4 %all-reduce.26.cloned.1.call-done = bf16[1024,224]{0,1:T(8,128)(2,1)} async-done(((bf16[1024,224]{0,1:T(8,128)(2,1)}), bf16[1024,224]{0,1:T(8,128)(2,1)}) %all-reduce.26.cloned.1.call-update) | async-done | bytes 458768 | tf_op jit(solution)/shard_map/psum | solution.py:64
  746.8 7.0 psum.123
  760.5 48.8 %reduce-scatter.41.cloned.1.call-done = bf16[256,2432]{1,0:T(8,128)(2,1)} async-done(((bf16[1024,2432]{1,0:T(8,128)(2,1)}), bf16[256,2432]{1,0:T(8,128)(2,1)}) %reduce-scatter.41.cloned.1.call-update) | async-done | bytes 1245200 | tf_op jit(solution)/shard_map/reduce_scatter | solution.py:72
  815.2 67.3 %all-gather.15.cloned.1.call-done = bf16[1024,4864]{1,0:T(8,128)(2,1)} async-done(((bf16[256,4864]{1,0:T(8,128)(2,1)}), bf16[1024,4864]{1,0:T(8,128)(2,1)}) %all-gather.15.cloned.1.call-update) | async-done | bytes 9961488 | tf_op jit(solution)/shard_map/all_gather | solution.py:68
  882.5 7.6 convolution_convert_fusion.12
  890.2 27.3 %all-reduce.28.cloned.1.call-done = bf16[1024,224]{0,1:T(8,128)(2,1)} async-done(((bf16[1024,224]{0,1:T(8,128)(2,1)}), bf16[1024,224]{0,1:T(8,128)(2,1)}) %all-reduce.28.cloned.1.call-update) | async-done | bytes 458768 | tf_op jit(solution)/shard_map/psum | solution.py:64
  918.9 6.9 psum.125
  931.3 23.2 %reduce-scatter.43.cloned.1.call-done = bf16[256,448]{0,1:T(8,128)(2,1)} async-done(((bf16[1024,448]{0,1:T(8,128)(2,1)}), bf16[256,448]{0,1:T(8,128)(2,1)}) %reduce-scatter.43.cloned.1.call-update) | async-done | bytes 229392 | tf_op jit(solution)/shard_map/reduce_scatter | solution.py:72
  975.6 16.4 %reduce-scatter.45.cloned.1.call-done = bf16[256,128]{0,1:T(8,128)(2,1)} async-done(((bf16[1024,128]{0,1:T(8,128)(2,1)}), bf16[256,128]{0,1:T(8,128)(2,1)}) %reduce-scatter.45.cloned.1.call-update) | async-done | bytes 65552 | tf_op jit(solution)/shard_map/reduce_scatter | solution.py:221
  993.8 39.2 %all-gather.9.cloned.1.call-done = bf16[1024,2432]{1,0:T(8,128)(2,1)} async-done(((bf16[256,2432]{1,0:T(8,128)(2,1)}), bf16[1024,2432]{1,0:T(8,128)(2,1)}) %all-gather.9.cloned.1.call-update) | async-done | bytes 4980752 | tf_op jit(solution)/shard_map/all_gather | solution.py:68
  1038.4 7.9 convolution_convert_fusion.2
  1057.5 8.1 convolution_convert_fusion.3
  1086.5 45.8 %reduce-scatter.53.cloned.1.call-done = bf16[56,4864]{1,0:T(8,128)(2,1)} async-done(((bf16[224,4864]{1,0:T(8,128)(2,1)}), bf16[56,4864]{1,0:T(8,128)(2,1)}) %reduce-scatter.53.cloned.1.call-update) | async-done | bytes 544784 | tf_op jit(solution)/shard_map/reduce_scatter | solution.py:250
  1135.0 29.4 %reduce-scatter.55.cloned.1.call-done = bf16[608,224]{1,0:T(8,128)(2,1)} async-done(((bf16[2432,224]{1,0:T(8,128)(2,1)}), bf16[608,224]{1,0:T(8,128)(2,1)}) %reduce-scatter.55.cloned.1.call-update) | async-done | bytes 272400
  1166.7 18.7 %reduce-scatter.49.cloned.1.call-done = bf16[112,224]{1,0:T(8,128)(2,1)} async-done(((bf16[448,224]{1,0:T(8,128)(2,1)}), bf16[112,224]{1,0:T(8,128)(2,1)}) %reduce-scatter.49.cloned.1.call-update) | async-done | bytes 50192 | tf_op jit(solution)/shard_map/reduce_scatter | solution.py:247
  1185.4 20.6 %reduce-scatter.47.cloned.1.call-done = bf16[112,224]{1,0:T(8,128)(2,1)} async-done(((bf16[448,224]{1,0:T(8,128)(2,1)}), bf16[112,224]{1,0:T(8,128)(2,1)}) %reduce-scatter.47.cloned.1.call-update) | async-done | bytes 50192 | tf_op jit(solution)/shard_map/reduce_scatter | solution.py:247
  1207.5 44.4 %reduce-scatter.51.cloned.1.call-done = bf16[56,4864]{1,0:T(8,128)(2,1)} async-done(((bf16[224,4864]{1,0:T(8,128)(2,1)}), bf16[56,4864]{1,0:T(8,128)(2,1)}) %reduce-scatter.51.cloned.1.call-update) | async-done | bytes 544784 | tf_op jit(solution)/shard_map/reduce_scatter | solution.py:250
  1259.2 15.4 %reduce-scatter.61.cloned.1.call-done = bf16[56,576]{1,0:T(8,128)(2,1)} async-done(((bf16[224,576]{1,0:T(8,128)(2,1)}), bf16[56,576]{1,0:T(8,128)(2,1)}) %reduce-scatter.61.cloned.1.call-update) | async-done | bytes 64528
  1274.6 20.8 %reduce-scatter.59.cloned.1.call-done = bf16[56,576]{1,0:T(8,128)(2,1)} async-done(((bf16[224,576]{1,0:T(8,128)(2,1)}), bf16[56,576]{1,0:T(8,128)(2,1)}) %reduce-scatter.59.cloned.1.call-update) | async-done | bytes 64528
  1297.1 36.6 %all-reduce.30.cloned.1.call-done = (bf16[1024,224]{0,1:T(8,128)(2,1)}, bf16[1024,224]{0,1:T(8,128)(2,1)}) async-done(((bf16[1024,224]{0,1:T(8,128)(2,1)}, bf16[1024,224]{0,1:T(8,128)(2,1)}), (bf16[1024,224]{0,1:T(8,128)(2,1)}, bf16[1024,224]{0,1:T(8,128)(2,1)})) %all-reduce.30.cloned.1.call-update) | async-done | bytes 917520 | tf_op jit(solution)/shard_map/psum | solution.py:64
  1337.0 11.8 all-reduce.8
  (384 shorter events, 209.6 us)
Async XLA Ops:
  7.2 40.9 %reduce-scatter.27.cloned.1.call-start = ((), (), s32[]{:S(2)}) async-start(), calls=%async_computation.18 | async-start | bytes 1474560 | tf_op jit(solution)/shard_map/reduce_scatter | solution.py:72
  18.0 90.7 %copy-start.79 = (f32[1,1,224]{2,1,0:T(1,128)}, f32[1,1,224]{2,1,0:T(1,128)S(1)}, u32[]{:S(2)}) copy-start(f32[1,1,224]{2,1,0:T(1,128)S(1)} %get-tuple-element.66) | copy-start | bytes 2692
  18.0 265.0 %copy-start.77 = (f32[1,1,224]{2,1,0:T(1,128)}, f32[1,1,224]{2,1,0:T(1,128)S(1)}, u32[]{:S(2)}) copy-start(f32[1,1,224]{2,1,0:T(1,128)S(1)} %get-tuple-element.68) | copy-start | bytes 2692
  21.9 78.1 %all-reduce.18.cloned.1.call-start = ((), (), s32[]{:S(2)}) async-start(), calls=%async_computation.19 | async-start | bytes 917504 | tf_op jit(solution)/shard_map/psum | solution.py:64
  23.6 287.3 %copy-start.85 = (f32[32]{0:T(128)}, f32[32]{0:T(128)S(1)}, u32[]{:S(2)}) copy-start(f32[32]{0:T(128)S(1)} %multiply_power_fusion) | copy-start | bytes 388
  24.4 286.5 %copy-start.65 = (f32[1,256]{1,0:T(1,128)}, f32[1,256]{1,0:T(1,128)S(1)}, u32[]{:S(2)}) copy-start(f32[1,256]{1,0:T(1,128)S(1)} %fusion.189) | copy-start | bytes 3076
  72.7 123.9 %reduce-scatter.29.cloned.1.call-start = ((), (), s32[]{:S(2)}) async-start(), calls=%async_computation.20 | async-start | bytes 12451840 | tf_op jit(solution)/shard_map/reduce_scatter | solution.py:72
  115.4 126.4 %all-gather.7.cloned.1.call-start = ((), (), s32[]{:S(2)}) async-start(), calls=%async_computation.21 | async-start | bytes 6225920 | tf_op jit(solution)/shard_map/all_gather | solution.py:68
  202.7 80.4 %copy-start.30 = (bf16[2,224,576]{2,1,0:T(8,128)(2,1)S(1)}, bf16[2,224,576]{2,1,0:T(8,128)(2,1)}, u32[]{:S(2)}) copy-start(bf16[2,224,576]{2,1,0:T(8,128)(2,1)} %param.11) | copy-start | bytes 1548292
  202.7 71.6 %all-reduce.20.cloned.1.call-start = ((), (), s32[]{:S(2)}) async-start(), calls=%async_computation.22 | async-start | bytes 917504 | tf_op jit(solution)/shard_map/psum | solution.py:64
  247.0 62.7 %reduce-scatter.31.cloned.1.call-start = ((), (), s32[]{:S(2)}) async-start(), calls=%async_computation.23 | async-start | bytes 1474560 | tf_op jit(solution)/shard_map/reduce_scatter | solution.py:72
  275.6 85.1 %copy-start.9 = (f32[1024,224]{0,1:T(8,128)}, f32[1024,224]{0,1:T(8,128)S(1)}, u32[]{:S(2)}) copy-start(f32[1024,224]{0,1:T(8,128)S(1)} %get-tuple-element.29) | copy-start | bytes 2752516
  284.7 76.0 %all-reduce.22.cloned.1.call-start = ((), (), s32[]{:S(2)}) async-start(), calls=%async_computation.24 | async-start | bytes 917504 | tf_op jit(solution)/shard_map/psum | solution.py:64
  317.0 345.0 %copy-start.38 = (bf16[1024,128]{0,1:T(8,128)(2,1)}, bf16[1024,128]{0,1:T(8,128)(2,1)S(1)}, u32[]{:S(2)}) copy-start(bf16[1024,128]{0,1:T(8,128)(2,1)S(1)} %all_gather.33) | copy-start | bytes 786436
  333.3 124.3 %reduce-scatter.33.cloned.1.call-start = ((), (), s32[]{:S(2)}) async-start(), calls=%async_computation.25 | async-start | bytes 12451840 | tf_op jit(solution)/shard_map/reduce_scatter | solution.py:72
  376.5 133.5 %reduce-scatter.35.cloned.1.call-start = ((), (), s32[]{:S(2)}) async-start(), calls=%async_computation.27 | async-start | bytes 6225920 | tf_op jit(solution)/shard_map/reduce_scatter | solution.py:72
  382.3 202.1 %all-gather.11.cloned.1.call-start = ((), (), s32[]{:S(2)}) async-start(), calls=%async_computation.28 | async-start | bytes 12451840 | tf_op jit(solution)/shard_map/all_gather | solution.py:68
  517.1 102.3 %all-reduce.24.cloned.1.call-start = ((), (), s32[]{:S(2)}) async-start(), calls=%async_computation.29 | async-start | bytes 917504 | tf_op jit(solution)/shard_map/psum | solution.py:64
  592.1 65.4 %reduce-scatter.37.cloned.1.call-start = ((), (), s32[]{:S(2)}) async-start(), calls=%async_computation.30 | async-start | bytes 1146880 | tf_op jit(solution)/shard_map/reduce_scatter | solution.py:72
  634.2 60.8 %reduce-scatter.39.cloned.1.call-start = ((), (), s32[]{:S(2)}) async-start(), calls=%async_computation.31 | async-start | bytes 327680 | tf_op jit(solution)/shard_map/reduce_scatter | solution.py:221
  674.8 40.6 %all-gather.13.cloned.1.call-start = ((), (), s32[]{:S(2)}) async-start(), calls=%async_computation.32 | async-start | bytes 1474560 | tf_op jit(solution)/shard_map/all_gather | solution.py:68
  677.7 76.1 %copy-start.7 = (f32[1024,224]{0,1:T(8,128)S(1)}, f32[1024,224]{0,1:T(8,128)}, u32[]{:S(2)}) copy-start(f32[1024,224]{0,1:T(8,128)} %copy-done.6) | copy-start | bytes 2752516
  677.7 76.1 %copy-start.24 = (bf16[1,1024,224]{1,2,0:T(8,128)(2,1)S(1)}, bf16[1,1024,224]{1,2,0:T(8,128)(2,1)}, u32[]{:S(2)}) copy-start(bf16[1,1024,224]{1,2,0:T(8,128)(2,1)} %param.17) | copy-start | bytes 1376260
  677.7 76.1 %copy-start.27 = (bf16[1024,224]{0,1:T(8,128)(2,1)S(1)}, bf16[1024,224]{0,1:T(8,128)(2,1)}, u32[]{:S(2)}) copy-start(bf16[1024,224]{0,1:T(8,128)(2,1)} %all-reduce.24.cloned.1.call-done) | copy-start | bytes 1376260
  697.6 47.8 %all-reduce.26.cloned.1.call-start = ((), (), s32[]{:S(2)}) async-start(), calls=%async_computation.33 | async-start | bytes 917504 | tf_op jit(solution)/shard_map/psum | solution.py:64
  718.0 91.3 %reduce-scatter.41.cloned.1.call-start = ((), (), s32[]{:S(2)}) async-start(), calls=%async_computation.34 | async-start | bytes 6225920 | tf_op jit(solution)/shard_map/reduce_scatter | solution.py:72
  760.4 122.1 %all-gather.15.cloned.1.call-start = ((), (), s32[]{:S(2)}) async-start(), calls=%async_computation.35 | async-start | bytes 12451840 | tf_op jit(solution)/shard_map/all_gather | solution.py:68
  815.1 102.4 %copy-start.4 = (bf16[1,1024,224]{1,2,0:T(8,128)(2,1)S(1)}, bf16[1,1024,224]{1,2,0:T(8,128)(2,1)}, u32[]{:S(2)}) copy-start(bf16[1,1024,224]{1,2,0:T(8,128)(2,1)} %param.9) | copy-start | bytes 1376260
  815.1 102.3 %copy-start.17 = (bf16[1024,224]{0,1:T(8,128)(2,1)S(1)}, bf16[1024,224]{0,1:T(8,128)(2,1)}, u32[]{:S(2)}) copy-start(bf16[1024,224]{0,1:T(8,128)(2,1)} %all-reduce.18.cloned.1.call-done) | copy-start | bytes 1376260
  815.1 102.3 %copy-start.57 = (f32[1024]{0:T(1024)S(1)}, f32[1024]{0:T(1024)}, u32[]{:S(2)}) copy-start(f32[1024]{0:T(1024)} %copy-done.56) | copy-start | bytes 12292
  815.1 102.3 %copy-start.80 = (f32[1,1,224]{2,1,0:T(1,128)S(1)}, f32[1,1,224]{2,1,0:T(1,128)}, u32[]{:S(2)}) copy-start(f32[1,1,224]{2,1,0:T(1,128)} %copy-done.79) | copy-start | bytes 2692
  815.1 110.6 %copy-start.84 = (f32[1024]{0:T(1024)S(1)}, f32[1024]{0:T(1024)}, u32[]{:S(2)}) copy-start(f32[1024]{0:T(1024)} %get-tuple-element.59) | copy-start | bytes 12292
  815.2 102.3 %all-reduce.28.cloned.1.call-start = ((), (), s32[]{:S(2)}) async-start(), calls=%async_computation.36 | async-start | bytes 917504 | tf_op jit(solution)/shard_map/psum | solution.py:64
  890.2 64.3 %reduce-scatter.43.cloned.1.call-start = ((), (), s32[]{:S(2)}) async-start(), calls=%async_computation.37 | async-start | bytes 1146880 | tf_op jit(solution)/shard_map/reduce_scatter | solution.py:72
  931.2 60.7 %reduce-scatter.45.cloned.1.call-start = ((), (), s32[]{:S(2)}) async-start(), calls=%async_computation.38 | async-start | bytes 327680 | tf_op jit(solution)/shard_map/reduce_scatter | solution.py:221
  971.7 61.3 %all-gather.9.cloned.1.call-start = ((), (), s32[]{:S(2)}) async-start(), calls=%async_computation.26 | async-start | bytes 6225920 | tf_op jit(solution)/shard_map/all_gather | solution.py:68
  972.4 96.0 %all-gather.17.cloned.1.call-start = ((), (), s32[]{:S(2)}) async-start(), calls=%async_computation.39 | async-start | bytes 1474560 | tf_op jit(solution)/shard_map/all_gather | solution.py:68
  993.7 91.6 %reduce-scatter.57.cloned.1.call-start = ((), (), s32[]{:S(2)}) async-start(), calls=%async_computation.45 | async-start | bytes 1556480
  1038.4 94.0 %reduce-scatter.53.cloned.1.call-start = ((), (), s32[]{:S(2)}) async-start(), calls=%async_computation.43 | async-start | bytes 2723840 | tf_op jit(solution)/shard_map/reduce_scatter | solution.py:250
  1046.4 118.1 %reduce-scatter.55.cloned.1.call-start = ((), (), s32[]{:S(2)}) async-start(), calls=%async_computation.44 | async-start | bytes 1556480
  1053.7 131.7 %reduce-scatter.49.cloned.1.call-start = ((), (), s32[]{:S(2)}) async-start(), calls=%async_computation.41 | async-start | bytes 286720 | tf_op jit(solution)/shard_map/reduce_scatter | solution.py:247
  1056.2 149.7 %reduce-scatter.47.cloned.1.call-start = ((), (), s32[]{:S(2)}) async-start(), calls=%async_computation.40 | async-start | bytes 286720 | tf_op jit(solution)/shard_map/reduce_scatter | solution.py:247
  1057.5 194.4 %reduce-scatter.51.cloned.1.call-start = ((), (), s32[]{:S(2)}) async-start(), calls=%async_computation.42 | async-start | bytes 2723840 | tf_op jit(solution)/shard_map/reduce_scatter | solution.py:250
  1065.7 208.9 %reduce-scatter.61.cloned.1.call-start = ((), (), s32[]{:S(2)}) async-start(), calls=%async_computation.47 | async-start | bytes 358400
  1068.4 227.0 %reduce-scatter.59.cloned.1.call-start = ((), (), s32[]{:S(2)}) async-start(), calls=%async_computation.46 | async-start | bytes 358400
  1071.2 262.5 %all-reduce.30.cloned.1.call-start = ((), (), s32[]{:S(2)}) async-start(), calls=%async_computation.48 | async-start | bytes 1835008 | tf_op jit(solution)/shard_map/psum | solution.py:64
  1253.9 83.1 %copy-start.89 = (bf16[224]{0:T(256)(128)(2,1)S(1)}, bf16[224]{0:T(256)(128)(2,1)}, u32[]{:S(2)}) copy-start(bf16[224]{0:T(256)(128)(2,1)} %get-tuple-element.12) | copy-start | bytes 1348
  1253.9 102.1 %copy-start.83 = (f32[1024]{0:T(1024)S(1)}, f32[1024]{0:T(1024)}, u32[]{:S(2)}) copy-start(f32[1024]{0:T(1024)} %get-tuple-element.57) | copy-start | bytes 12292
  (78 other events, 1401.9 us)
Sparse Core Ops, SparseCore 0:
  22.1 26.0 reduce-scatter.26
  72.8 27.1 all-reduce.17
  115.6 80.9 reduce-scatter.28
  202.8 38.9 all-gather.6
  247.1 27.1 all-reduce.19
  284.8 24.8 reduce-scatter.30
  333.5 27.1 all-reduce.21
  376.6 80.9 reduce-scatter.32
  460.3 49.6 reduce-scatter.34
  517.2 67.2 all-gather.10
  592.2 27.1 all-reduce.23
  634.3 23.1 reduce-scatter.36
  674.9 20.0 reduce-scatter.38
  697.8 17.5 all-gather.12
  718.2 27.1 all-reduce.25
  760.6 48.7 reduce-scatter.40
  815.2 67.2 all-gather.14
  890.3 27.1 all-reduce.27
  931.3 23.1 reduce-scatter.42
  971.8 20.0 reduce-scatter.44
  994.1 38.9 all-gather.8
  1035.1 17.5 all-gather.16
  1055.1 30.2 reduce-scatter.56
  1088.2 44.0 reduce-scatter.52
  1134.8 29.6 reduce-scatter.54
  1167.1 18.2 reduce-scatter.48
  1188.2 17.7 reduce-scatter.46
  1208.3 43.5 reduce-scatter.50
  1254.8 19.7 reduce-scatter.60
  1276.8 18.5 reduce-scatter.58
  1298.4 35.2 all-reduce.29
where the time goes:
time: 1380 us; the launch traced here: 1370 us
  waiting for transfers between devices  1000 us (72%)
  matrix products  127 us (9%)
  blocking collectives  98.3 us (7%)
  other arithmetic  80.8 us (6%)
  local copies, waits for them, and re-layouts  38.2 us (3%)
  between operations  17.5 us (1%)
    reduce_scatter x8, waiting for transfers between devices, row_products(): lax.psum_scatter(contract(values, weight, flipped).astype(jnp.bfloat16),...  345 us
    all_gather x6, waiting for transfers between devices, gather_rows(): return lax.all_gather(values, 'wid', axis=0, tiled=True)  230 us
    psum x7, waiting for transfers between devices, head_total(): lax.psum(partial_rows.astype(jnp.bfloat16), 'grp').astype(jnp.float32)  191 us
    reduce_scatter x2, waiting for transfers between devices, layer_backward(): lax.psum_scatter(grad_gate_w.astype(jnp.bfloat16), 'dp', scatter_dimensio...  90.2 us
    unnamed x35, waiting for transfers between devices  72.1 us
    psum x8, blocking collectives, width_total(): return lax.psum(vector, 'wid')  56.1 us
    reduce_scatter x2, waiting for transfers between devices, layer_backward(): lax.psum_scatter(grad_out_w.astype(jnp.bfloat16), 'dp', scatter_dimension...  39.3 us
    dot_general x8, matrix products, transposed_product(): lax.dot_general(left_side, right_side, (((0,), (0,)), ((), ())), preferre...  33.3 us
  transfers between devices with their start and end apart: 31, of which 30 were waited for; matrix products, arithmetic and copies ran while one was open for 7% of the time, Pallas kernels for 0%

commit v1 on v0

v1 whole, which is shorter than its diff:
```python
import functools

import jax
import jax.numpy as jnp
from jax import lax
from jax.experimental import pallas as pl
from jax.experimental.pallas import tpu as pltpu
from jax.sharding import PartitionSpec as P

D = 896
HEADS = 14
KV_HEADS = 2
HEAD_DIM = 64
LAYERS = 2
PER = HEADS // KV_HEADS
QW = PER * HEAD_DIM

EPSILON = 1e-06
ROPE_BASE = 1000000.0
NEGATIVE = -1e30
MESH = pl.DeviceIdType.MESH
LOW = jnp.bfloat16
VMEM = pl.BlockSpec(memory_space=pltpu.VMEM)
LIMIT = 48 * 1024 * 1024


def place():
    return lax.axis_index("wid"), lax.axis_index("grp")


def flip_core(w):
    return w + 1 - 2 * lax.rem(w, 2)


def flip_far(w):
    return lax.rem(w + 2, 4)


def meet(devices):
    barrier = pltpu.get_barrier_semaphore()
    for device in devices:
        pl.semaphore_signal(barrier, inc=1, device_id=device, device_id_type=MESH)
    pl.semaphore_wait(barrier, len(devices))


def partners(kind):
    w, g = place()
    if kind == "grp":
        return g, [({"grp": 1 - g}, 1 - g)]
    ws = [flip_core(w), flip_far(w), flip_far(flip_core(w))]
    if kind == "wid":
        return w, [({"wid": v}, v) for v in ws]
    listed = [({"wid": v, "grp": 1 - g}, v * 2 + 1 - g) for v in [w] + ws]
    listed += [({"wid": v, "grp": g}, v * 2 + g) for v in ws]
    return w * 2 + g, listed


def send(src, dst, ss, rs, device):
    copy = pltpu.make_async_remote_copy(
        src_ref=src, dst_ref=dst, send_sem=ss, recv_sem=rs, device_id=device, device_id_type=MESH
    )
    copy.start()
    return copy


def swap_kernel(kind, gather, x, o, ss, rs):
    me, others = partners(kind)
    meet([d for d, _ in others])
    copies = []
    for j, (device, slot) in enumerate(others):
        src = x if gather else x.at[slot]
        copies.append(send(src, o.at[me], ss.at[j], rs.at[j], device))
    o[me] = x[...] if gather else x[me]
    for copy in copies:
        copy.wait()


def sum_kernel(kind, x, o, buf, ss, rs):
    me, others = partners(kind)
    meet([d for d, _ in others])
    copies = []
    for j, (device, slot) in enumerate(others):
        copies.append(send(x.at[slot], buf.at[j], ss.at[j], rs.at[j], device))
    total = x[me].astype(jnp.float32)
    for j, copy in enumerate(copies):
        copy.wait()
        total = total + buf[j].astype(jnp.float32)
    o[...] = total


def relations():
    w, g = place()
    s = flip_core(w)
    f, fs = flip_far(w), flip_far(s)
    mine = [(w, g), (f, 1 - g), (f, g), (w, 1 - g)]
    theirs = [(s, g), (fs, 1 - g), (fs, g), (s, 1 - g)]
    return mine, theirs


def dev(pair):
    return {"wid": pair[0], "grp": pair[1]}


def slot_of(pair):
    return pair[0] * 2 + pair[1]


def gather_kernel(x, o, ss, rs):
    mine, theirs = relations()
    sibling = dev(theirs[0])
    meet([sibling] + [dev(p) for p in mine[1:]])
    me = slot_of(mine[0])
    copies = [send(x, o.at[me], ss.at[j], rs.at[j], dev(mine[j])) for j in (1, 2, 3)]
    near = send(x, o.at[me], ss.at[0], rs.at[0], sibling)
    o[me] = x[...]
    passed = []
    for j in (2, 3, 1):
        copies[j - 1].wait_recv()
        at = slot_of(mine[j])
        passed.append(send(o.at[at], o.at[at], ss.at[3 + j], rs.at[3 + j], sibling))
    near.wait()
    for j in (1, 2, 3):
        copies[j - 1].wait_send()
    for copy in passed:
        copy.wait()


def scatter_kernel(x, o, first, outgo, second, ss, rs):
    mine, theirs = relations()
    sibling = dev(theirs[0])
    meet([sibling] + [dev(p) for p in mine[1:]])
    order = (1, 2, 3, 0)
    shared = {j: send(x.at[slot_of(theirs[j])], first.at[j], ss.at[j], rs.at[j], sibling) for j in order}
    sent = {}
    for j in (1, 2, 3):
        shared[j].wait_recv()
        pair = x[slot_of(mine[j])].astype(jnp.float32) + first[j].astype(jnp.float32)
        outgo[j - 1] = pair.astype(LOW)
        sent[j] = send(outgo.at[j - 1], second.at[j - 1], ss.at[3 + j], rs.at[3 + j], dev(mine[j]))
    shared[0].wait_recv()
    total = x[slot_of(mine[0])].astype(jnp.float32) + first[0].astype(jnp.float32)
    for j in (2, 3, 1):
        sent[j].wait_recv()
        total = total + second[j - 1].astype(jnp.float32)
    o[...] = total
    for j in order:
        shared[j].wait_send()
    for j in (1, 2, 3):
        sent[j].wait_send()


class Links:
    def __init__(self):
        self.ids = {}

    def call(self, key, kernel, out, scratch, x):
        number = self.ids.setdefault((key, x.shape, str(x.dtype)), len(self.ids))
        return pl.pallas_call(
            kernel,
            out_shape=out,
            in_specs=[VMEM],
            out_specs=VMEM,
            scratch_shapes=scratch,
            compiler_params=pltpu.CompilerParams(
                collective_id=number, has_side_effects=True, vmem_limit_bytes=LIMIT
            ),
        )(x)

    def swap(self, kind, x, gather=False):
        n = {"grp": 2, "wid": 4, "all": 8}[kind]
        shape = (n,) + x.shape if gather else x.shape
        sems = [pltpu.SemaphoreType.DMA((n - 1,))] * 2
        kernel = functools.partial(swap_kernel, kind, gather)
        return self.call(("swap", kind, gather), kernel, jax.ShapeDtypeStruct(shape, x.dtype), sems, x)

    def total(self, kind, x):
        n = x.shape[0]
        scratch = [pltpu.VMEM((n - 1,) + x.shape[1:], x.dtype)]
        scratch += [pltpu.SemaphoreType.DMA((n - 1,))] * 2
        kernel = functools.partial(sum_kernel, kind)
        out = jax.ShapeDtypeStruct(x.shape[1:], jnp.float32)
        return self.call(("sum", kind), kernel, out, scratch, x)

    def gather_all(self, x):
        sems = [pltpu.SemaphoreType.DMA((7,))] * 2
        out = jax.ShapeDtypeStruct((8,) + x.shape, x.dtype)
        return self.call("gather", gather_kernel, out, sems, x).reshape(-1, x.shape[-1])

    def scatter_all(self, x):
        x = x.reshape(8, -1, x.shape[-1])
        tail = x.shape[1:]
        scratch = [pltpu.VMEM((n,) + tail, x.dtype) for n in (4, 3, 3)]
        scratch += [pltpu.SemaphoreType.DMA((7,))] * 2
        out = jax.ShapeDtypeStruct(tail, jnp.float32)
        return self.call("scatter", scatter_kernel, out, scratch, x)


def permute_swap(x):
    n = x.shape[0]
    me = lax.axis_index("wid")
    out = x
    for k in range(1, n):
        other = jnp.bitwise_xor(me, k)
        piece = lax.dynamic_index_in_dim(x, other, 0, keepdims=True)
        piece = lax.ppermute(piece, "wid", [(i, i ^ k) for i in range(n)])
        out = lax.dynamic_update_slice_in_dim(out, piece, other, 0)
    return out


def dot(a, b, over):
    return lax.dot_general(a, b, ((over[0], over[1]), ((), ())), preferred_element_type=jnp.float32)


NN = ((1,), (0,))
NT = ((1,), (1,))
TN = ((0,), (0,))


def soften(q, k, bias):
    scores = dot(q, k, NT) + bias
    raised = jnp.exp(scores - jnp.max(scores, axis=-1, keepdims=True))
    return raised / jnp.sum(raised, axis=-1, keepdims=True)


def attend_kernel(q, kv, bias, o):
    k, v = kv[:, :HEAD_DIM], kv[:, HEAD_DIM:]
    for h in range(PER):
        cols = slice(h * HEAD_DIM, (h + 1) * HEAD_DIM)
        prob = soften(q[:, cols], k, bias[...]).astype(LOW)
        o[:, cols] = dot(prob, v, NN).astype(LOW)


def attend_back_kernel(q, kv, bias, do, dq, dkv):
    k, v = kv[:, :HEAD_DIM], kv[:, HEAD_DIM:]
    dk = jnp.zeros(k.shape, jnp.float32)
    dv = jnp.zeros(k.shape, jnp.float32)
    for h in range(PER):
        cols = slice(h * HEAD_DIM, (h + 1) * HEAD_DIM)
        qh, doh = q[:, cols], do[:, cols]
        soft = soften(qh, k, bias[...])
        dprob = dot(doh, v, NT)
        inner = jnp.sum(soft * dprob, axis=-1, keepdims=True)
        ds = (soft * (dprob - inner)).astype(LOW)
        dq[:, cols] = dot(ds, k, NN) * HEAD_DIM ** (-0.5)
        dk = dk + dot(ds, qh, TN)
        dv = dv + dot(soft.astype(LOW), doh, TN)
    dkv[:, :HEAD_DIM] = dk.astype(LOW)
    dkv[:, HEAD_DIM:] = dv.astype(LOW)


def local_call(kernel, out, args, flops):
    return pl.pallas_call(
        kernel,
        out_shape=out,
        in_specs=[VMEM] * len(args),
        out_specs=jax.tree.map(lambda _: VMEM, out),
        compiler_params=pltpu.CompilerParams(vmem_limit_bytes=LIMIT),
        cost_estimate=pl.CostEstimate(flops=flops, bytes_accessed=4_000_000, transcendentals=2_000_000),
    )(*args)


def rope_tables(doc_ids, offset, span_rows):
    position_grid = lax.broadcasted_iota(jnp.int32, doc_ids.shape, 1)
    change = jnp.concatenate(
        [jnp.ones_like(doc_ids[:, :1]), (doc_ids[:, 1:] != doc_ids[:, :-1]).astype(jnp.int32)],
        axis=1,
    )
    starts = lax.cummax(jnp.where(change > 0, position_grid, 0), axis=1)
    places = (position_grid - starts).astype(jnp.float32)
    places = jnp.transpose(lax.dynamic_slice_in_dim(places, offset, span_rows, 1))
    frequency = ROPE_BASE ** (-jnp.arange(HEAD_DIM // 2, dtype=jnp.float32) / (HEAD_DIM // 2))
    angles = places * frequency[None, :]
    cosine, sine = jnp.cos(angles), jnp.sin(angles)
    still = jnp.ones((span_rows, HEAD_DIM), jnp.float32)
    cosine_all = jnp.concatenate([cosine] * (2 * (PER + 1)) + [still], axis=1)
    sine_all = jnp.concatenate([-sine, sine] * (PER + 1) + [still * 0.0], axis=1)
    return cosine_all, sine_all


def rotate(values, cosine_all, sine_all):
    half = HEAD_DIM // 2
    lane = lax.broadcasted_iota(jnp.int32, values.shape, 1)
    turned = jnp.where(
        lane % HEAD_DIM < half, jnp.roll(values, -half, axis=1), jnp.roll(values, half, axis=1)
    )
    return values * cosine_all + turned * sine_all


def normalize(values, gain_row):
    scale_rows = lax.rsqrt(jnp.sum(values * values, axis=1, keepdims=True) / D + EPSILON)
    return ((values * scale_rows * gain_row).astype(LOW), scale_rows)


def normalize_back(values, gain_row, scale_rows, grad_norm):
    inner_sum = jnp.sum(grad_norm * gain_row * values, axis=1, keepdims=True)
    grad_values = grad_norm * gain_row * scale_rows - values * scale_rows**3 * inner_sum / D
    grad_gain = jnp.sum(grad_norm * values * scale_rows, axis=0)
    return (grad_values, grad_gain)


def per_device(
    hidden_in,
    doc_ids,
    qkv_weight,
    qkv_bias,
    out_weight,
    gate_up,
    down_weight,
    norm_gains,
    cotangent,
):
    _, length, own = hidden_in.shape
    nw, ng, nd = lax.axis_size("wid"), lax.axis_size("grp"), lax.axis_size("dp")
    w, g = place()
    span = length // nw
    rows = span // ng
    ff = down_weight.shape[1]
    part = ff // nw
    offset = w * span
    links = Links()

    weights = []
    gains = lax.all_gather(norm_gains, "wid", axis=2, tiled=True)
    for n in range(LAYERS):
        qkv_w = lax.all_gather(qkv_weight[n], "wid", axis=0, tiled=True)
        out_w = lax.all_gather(out_weight[n], "wid", axis=1, tiled=True)
        both = gate_up[n].reshape(own, 2, nw, part).transpose(2, 1, 0, 3)
        both = permute_swap(both)
        gate_w = both[:, 0].reshape(D, part)
        up_w = both[:, 1].reshape(D, part)
        down_w = permute_swap(down_weight[n].reshape(nw, part, own))
        down_w = down_w.transpose(1, 0, 2).reshape(part, D)
        weights.append((qkv_w, out_w, gate_w, up_w, down_w))

    both = jnp.stack([hidden_in[0], cotangent[0]]).reshape(2, nw, ng, rows, own)
    both = lax.dynamic_index_in_dim(both, g, 2, keepdims=False)
    both = both.transpose(1, 0, 2, 3).reshape(nw, 2 * rows, own)
    both = links.swap("wid", both).transpose(1, 0, 2).reshape(2, rows, D).astype(jnp.float32)
    h, grad = both[0], both[1]

    cosine_all, sine_all = rope_tables(doc_ids, offset, span)
    query_doc = lax.dynamic_slice_in_dim(doc_ids[0], offset, span, 0)
    query_place = offset + lax.iota(jnp.int32, span)
    key_place = lax.iota(jnp.int32, length)
    allowed = (key_place[None, :] <= query_place[:, None]) & (query_doc[:, None] == doc_ids[0][None, :])
    bias = jnp.where(allowed, 0.0, NEGATIVE).astype(jnp.float32)
    scale_row = jnp.concatenate(
        [jnp.full((QW,), HEAD_DIM ** (-0.5), jnp.float32), jnp.ones((2 * HEAD_DIM,), jnp.float32)]
    )
    flops = 4 * PER * span * length * HEAD_DIM

    stored = []
    for n in range(LAYERS):
        qkv_w, out_w, gate_w, up_w, down_w = weights[n]
        a1, r1 = normalize(h, gains[n, 0])
        a1 = links.swap("grp", a1, gather=True).reshape(span, D)
        p = dot(a1, qkv_w, NN) + qkv_bias[n]
        p = (rotate(p, cosine_all, sine_all) * scale_row).astype(LOW)
        q, kv = p[:, :QW], p[:, QW:]
        kv = links.swap("wid", kv, gather=True).reshape(length, 2 * HEAD_DIM)
        o = local_call(
            attend_kernel, jax.ShapeDtypeStruct(q.shape, LOW), (q, kv, bias), flops
        )
        y = dot(o, out_w, NN).astype(LOW).reshape(ng, rows, D)
        h1 = h + links.total("grp", y)
        a2, r2 = normalize(h1, gains[n, 1])
        a2 = links.gather_all(a2)
        gate = dot(a2, gate_w, NN)
        up = dot(a2, up_w, NN)
        m = (jax.nn.silu(gate) * up).astype(LOW)
        gate, up = gate.astype(LOW), up.astype(LOW)
        z = links.scatter_all(dot(m, down_w, NN).astype(LOW))
        stored.append((h, a1, r1, q, kv, o, h1, r2, a2, gate, up, m))
        h = h1 + z

    def to_width(values):
        pieces = values.astype(LOW).reshape(rows, nw, own).transpose(1, 0, 2)
        pieces = jnp.broadcast_to(pieces[:, None], (nw, ng, rows, own)).reshape(nw * ng, rows, own)
        return links.swap("all", pieces).reshape(1, length, own)

    hidden_out = to_width(h)

    grads = []
    small = []
    for n in reversed(range(LAYERS)):
        qkv_w, out_w, gate_w, up_w, down_w = weights[n]
        h, a1, r1, q, kv, o, h1, r2, a2, gate, up, m = stored[n]
        gz = links.gather_all(grad.astype(LOW))
        dm = dot(gz, down_w, NT)
        gate, up = gate.astype(jnp.float32), up.astype(jnp.float32)
        sig = jax.nn.sigmoid(gate)
        dgate = (dm * up * sig * (1.0 + gate * (1.0 - sig))).astype(LOW)
        dup = (dm * (gate * sig)).astype(LOW)
        da2 = links.scatter_all((dot(dgate, gate_w, NT) + dot(dup, up_w, NT)).astype(LOW))
        down_g = dot(m, gz, TN).astype(LOW)
        gate_g = jnp.stack([dot(a2, dgate, TN).astype(LOW), dot(a2, dup, TN).astype(LOW)])
        down_g = permute_swap(down_g.reshape(part, nw, own).transpose(1, 0, 2)).reshape(ff, own)
        down_g = lax.psum_scatter(down_g, "dp", scatter_dimension=0, tiled=True).astype(jnp.float32)
        gate_g = gate_g.reshape(2, nw, nd, own // nd, part).transpose(2, 1, 3, 0, 4)
        gate_g = gate_g.reshape(nd * nw * (own // nd), 2 * part)
        gate_g = lax.psum_scatter(gate_g, "dp", scatter_dimension=0, tiled=True)
        gate_g = permute_swap(gate_g.reshape(nw, own // nd, 2 * part))
        gate_g = gate_g.reshape(nw, own // nd, 2, part).transpose(1, 2, 0, 3)
        gate_g = gate_g.reshape(own // nd, 2, ff).astype(jnp.float32)

        back, gain_two = normalize_back(h1, gains[n, 1], r2, da2)
        g1 = grad + back
        gy = links.swap("grp", g1.astype(LOW), gather=True).reshape(span, D)
        do = dot(gy, out_w, NT).astype(LOW)
        dq, dkv = local_call(
            attend_back_kernel,
            (jax.ShapeDtypeStruct(q.shape, jnp.float32), jax.ShapeDtypeStruct(kv.shape, LOW)),
            (q, kv, bias, do),
            2 * flops,
        )
        dkv = links.total("wid", dkv.reshape(nw, span, 2 * HEAD_DIM))
        dp = rotate(jnp.concatenate([dq, dkv], axis=1), cosine_all, -sine_all).astype(LOW)
        da1 = links.total("grp", dot(dp, qkv_w, NT).astype(LOW).reshape(ng, rows, D))
        back, gain_one = normalize_back(h, gains[n, 0], r1, da1)
        grad = g1 + back

        out_g = dot(o, gy, TN).astype(LOW)
        out_g = out_g.reshape(QW, nw, own).transpose(1, 0, 2).reshape(nw * QW, own)
        out_g = lax.psum_scatter(out_g, ("wid", "dp"), scatter_dimension=0, tiled=True)
        qkv_g = lax.psum_scatter(
            dot(a1, dp, TN).astype(LOW), ("wid", "dp"), scatter_dimension=0, tiled=True
        )
        bias_g = jnp.sum(dp, axis=0, dtype=jnp.float32)
        bias_g = jnp.where(lax.iota(jnp.int32, ng)[:, None] == g, bias_g[None, :], 0.0).reshape(-1)
        small.append(jnp.concatenate([gain_one, gain_two, bias_g]))
        grads.append((qkv_g.astype(jnp.float32), out_g.astype(jnp.float32), gate_g, down_g))

    input_grad = to_width(grad).astype(jnp.float32)
    grads, small = grads[::-1], small[::-1]
    small = lax.psum(jnp.stack(small), ("dp", "grp", "wid"))
    at = lax.axis_index("dp")
    gain_g = small[:, : 2 * D].reshape(LAYERS, 2, D)
    gain_g = lax.dynamic_slice_in_dim(gain_g, w * own + at * (own // nd), own // nd, 2)
    bias_all = small[:, 2 * D :]
    width = bias_all.shape[1] // (ng * nd)
    bias_g = lax.dynamic_slice_in_dim(bias_all, (g * nd + at) * width, width, 1)
    return (
        hidden_out,
        input_grad,
        jnp.stack([member[0] for member in grads]),
        bias_g,
        jnp.stack([member[1] for member in grads]),
        jnp.stack([member[2] for member in grads]),
        jnp.stack([member[3] for member in grads]),
        gain_g,
    )


def solution(mesh):
    placed = (
        P("dp", None, "wid"),
        P("dp", None),
        P(None, "wid", "grp"),
        P(None, "grp"),
        P(None, "grp", "wid"),
        P(None, "wid", None, "grp"),
        P(None, "grp", "wid"),
        P(None, None, "wid"),
        P("dp", None, "wid"),
    )
    return jax.shard_map(
        per_device,
        mesh=mesh,
        in_specs=placed,
        out_specs=(
            P("dp", None, "wid"),
            P("dp", None, "wid"),
            P(None, ("wid", "dp"), "grp"),
            P(None, ("grp", "dp")),
            P(None, ("grp", "dp"), "wid"),
            P(None, ("wid", "dp"), None, "grp"),
            P(None, ("grp", "dp"), "wid"),
            P(None, None, ("wid", "dp")),
        ),
        check_vma=False,
    )
```

time: 1380 us -> 867 us (0.63)
  waiting for transfers between devices: 1000 us -> 214 us
  Pallas kernels: 0 us -> 271 us
  local copies, waits for them, and re-layouts: 38.2 us -> 149 us
  matrix products: 127 us -> 59.4 us
  other arithmetic: 80.8 us -> 21.8 us
  starting transfers between devices: 2.37 us -> 18.8 us
    reduce_scatter x14 -> x4, waiting for transfers between devices: 508 us -> 93.8 us  [the longest x2 93.8 us: per_device(): gate_g = lax.psum_scatter(gate_g, 'dp', scatter_dimension=0, tiled=True)]
    pallas_call x0 -> x27, Pallas kernels: none -> 271 us  [the longest x23 247 us: call(): pl.pallas_call(kernel, out_shape=out, in_specs=[VMEM], out_specs=VMEM, sc...]
    all_gather x6 -> x0, waiting for transfers between devices: 230 us -> none  [gather_rows(): return lax.all_gather(values, 'wid', axis=0, tiled=True)]
    psum x7 -> x0, waiting for transfers between devices: 191 us -> none  [head_total(): lax.psum(partial_rows.astype(jnp.bfloat16), 'grp').astype(jnp.float32)]
    dot_general x36 -> x30, matrix products: 127 us -> 59.4 us  [dot(): lax.dot_general(a, b, ((over[0], over[1]), ((), ())), preferred_element_t...]
    ppermute x0 -> x24, waiting for transfers between devices: none -> 58.7 us  [permute_swap(): piece = lax.ppermute(piece, 'wid', [(i, i ^ k) for i in range(n)])]
    all_gather x4 -> x5, blocking collectives: 30.4 us -> 70.3 us  [the longest x2 28.9 us: per_device(): out_w = lax.all_gather(out_weight[n], 'wid', axis=1, tiled=True)]
    another operation x27 -> x8, other arithmetic: 33.6 us -> 5.04 us  [the longest x1 1.65 us: per_device(): jnp.stack([member[0] for member in grads])]
  transfers between devices with their start and end apart: 31 -> 32, of which waited for: 30 -> 14; matrix products, arithmetic and copies ran while one was open for 7% -> 21% of each run, Pallas kernels for 0% -> 22%
where the time goes in v1:
time: 867 us; the launch traced here: 862 us
  Pallas kernels  271 us (31%)
  waiting for transfers between devices  214 us (25%)
  local copies, waits for them, and re-layouts  149 us (17%)
  blocking collectives  111 us (13%)
  matrix products  59.4 us (7%)
  other arithmetic  21.8 us (3%)
  starting transfers between devices  18.8 us (2%)
  between operations  16.5 us (2%)
    pallas_call x23, Pallas kernels, call(): pl.pallas_call(kernel, out_shape=out, in_specs=[VMEM], out_specs=VMEM, sc...  247 us
    reduce_scatter x2, waiting for transfers between devices, per_device(): gate_g = lax.psum_scatter(gate_g, 'dp', scatter_dimension=0, tiled=True)  93.8 us
    unnamed x12, waiting for transfers between devices  61.6 us
    dot_general x30, matrix products, dot(): lax.dot_general(a, b, ((over[0], over[1]), ((), ())), preferred_element_t...  59.4 us
    ppermute x24, waiting for transfers between devices, permute_swap(): piece = lax.ppermute(piece, 'wid', [(i, i ^ k) for i in range(n)])  58.7 us
    psum x1, blocking collectives, per_device(): small = lax.psum(jnp.stack(small), ('dp', 'grp', 'wid'))  40.2 us
    all_gather x2, blocking collectives, per_device(): out_w = lax.all_gather(out_weight[n], 'wid', axis=1, tiled=True)  28.9 us
    pallas_call x4, Pallas kernels, local_call(): pl.pallas_call(kernel, out_shape=out, in_specs=[VMEM] * len(args), out_sp...  24.6 us
  transfers between devices with their start and end apart: 32, of which 14 were waited for; matrix products, arithmetic and copies ran while one was open for 21% of the time, Pallas kernels for 22%

profile of v1, /device:TPU:0, one launch (start us, length us, event | category | flops | bytes accessed | tf_op | source)
XLA Modules:
  0.0 861.5 jit_solution(943528574347430278)
XLA Ops:
  20.1 19.4 %all_gather.15 = f32[2,2,896]{1,0,2:T(2,128)S(1)} all-gather(f32[2,2,224]{1,0,2:T(2,128)S(1)} %copy.242), channel_id=1, replica_groups=mesh['dp'=4,'grp'=2,'wid'=4] {'wid'}, dimensions={2}, use_global_device_ids=true | all-gather | bytes 17920 | tf_op jit(solution)/shard_map/all_gather | solution.py:323
  39.5 11.5 %slice_reduce_fusion = (f32[896]{0:T(1024)S(1)}, f32[896]{0:T(1024)S(1)}, f32[896]{0:T(1024)S(1)}, f32[896]{0:T(1024)S(1)}) fusion(f32[2,2,896]{1,0,2:T(2,128)S(1)} %all_gather.15), kind=kLoop, calls=%fused_computation.107 | loop fusion | bytes 28672 | tf_op jit(solution)/shard_map/slice | solution.py:366
  54.4 8.9 %shard_map.152 = bf16[4,256,224]{2,1,0:T(8,128)(2,1)S(1)} custom-call(bf16[4,256,224]{2,1,0:T(8,128)(2,1)S(1)} %bitcast.218), custom_call_target="tpu_custom_call" | custom-call | tf_op jit(solution)/shard_map/pallas_call | solution.py:158
  66.2 7.8 shard_map.153
  74.1 10.7 %all-gather = bf16[1,896,576]{2,1,0:T(8,128)(2,1)S(1)} all-gather(bf16[1,224,576]{2,1,0:T(8,128)(2,1)S(1)} %get-tuple-element.150), channel_id=2, replica_groups=mesh['dp'=4,'grp'=2,'wid'=4] {'wid'}, dimensions={1}, use_global_device_ids=true | all-gather | bytes 1290240 | tf_op jit(solution)/shard_map/all_gather | solution.py:325
  96.0 11.2 %all-gather.2 = bf16[1,896,576]{2,1,0:T(8,128)(2,1)} all-gather(bf16[1,224,576]{2,1,0:T(8,128)(2,1)S(1)} %get-tuple-element.149), channel_id=4, replica_groups=mesh['dp'=4,'grp'=2,'wid'=4] {'wid'}, dimensions={1}, use_global_device_ids=true | all-gather | bytes 1290240 | tf_op jit(solution)/shard_map/all_gather | solution.py:325
  107.2 5.4 shard_map.154
  112.6 14.8 %all-gather.1 = bf16[1,448,896]{1,0,2:T(2,128)(2,1)} all-gather(bf16[1,448,224]{1,0,2:T(2,128)(2,1)S(1)} %copy-done.48), channel_id=3, replica_groups=mesh['dp'=4,'grp'=2,'wid'=4] {'wid'}, dimensions={2}, use_global_device_ids=true | all-gather | bytes 1003520 | tf_op jit(solution)/shard_map/all_gather | solution.py:326
  127.5 5.3 copy.246
  137.9 7.9 shard_map.156
  146.7 14.1 %all-gather.3 = bf16[1,448,896]{1,0,2:T(2,128)(2,1)} all-gather(bf16[1,448,224]{1,0,2:T(2,128)(2,1)S(1)} %copy-done.47), channel_id=5, replica_groups=mesh['dp'=4,'grp'=2,'wid'=4] {'wid'}, dimensions={2}, use_global_device_ids=true | all-gather | bytes 1003520 | tf_op jit(solution)/shard_map/all_gather | solution.py:326
  160.8 6.2 fusion.59
  167.0 7.5 reshape_squeeze.28
  177.8 7.5 reshape_squeeze.24
  195.7 5.4 copy.258
  201.2 15.7 %shard_map.157 = bf16[8,128,896]{2,1,0:T(8,128)(2,1)S(1)} custom-call(bf16[128,896]{1,0:T(8,128)(2,1)S(1)} %multiply_convert_fusion.4.x), custom_call_target="tpu_custom_call" | custom-call | tf_op jit(solution)/shard_map/pallas_call | solution.py:158
  216.9 15.0 %shard_map.166 = bf16[8,128,896]{2,1,0:T(8,128)(2,1)S(1)} custom-call(bf16[128,896]{1,0:T(8,128)(2,1)S(1)} %convert_element_type.239.x), custom_call_target="tpu_custom_call" | custom-call | tf_op jit(solution)/shard_map/pallas_call | solution.py:158
  244.9 9.1 %collective-permute-done.1 = bf16[1,2,224,608]{3,2,0,1:T(8,128)(2,1)S(1)} collective-permute-done((bf16[1,2,224,608]{3,2,0,1:T(8,128)(2,1)}, bf16[1,2,224,608]{3,2,0,1:T(8,128)(2,1)S(1)}, u32[]{:S(2)}, u32[]{:S(2)}) %collective-permute-start.1) | collective-permute-done | bytes 544800 | tf_op jit(solution)/shard_map/ppermute | solution.py:205
  254.1 11.1 %collective-permute-done.2 = bf16[1,2,224,608]{3,2,0,1:T(8,128)(2,1)S(1)} collective-permute-done((bf16[1,2,224,608]{3,2,0,1:T(8,128)(2,1)S(1)}, bf16[1,2,224,608]{3,2,0,1:T(8,128)(2,1)S(1)}, u32[]{:S(2)}, u32[]{:S(2)}) %collective-permute-start.2) | collective-permute-done | bytes 544800 | tf_op jit(solution)/shard_map/ppermute | solution.py:205
  271.7 28.7 %shard_map.158 = f32[128,896]{1,0:T(8,128)S(1)} custom-call(bf16[8,128,896]{2,1,0:T(8,128)(2,1)S(1)} %bitcast.236), custom_call_target="tpu_custom_call" | custom-call | tf_op jit(solution)/shard_map/pallas_call | solution.py:158
  300.7 7.1 shard_map.159
  311.7 5.4 shard_map.160
  322.5 7.9 shard_map.162
  330.6 14.5 %shard_map.163 = bf16[8,128,896]{2,1,0:T(8,128)(2,1)S(1)} custom-call(bf16[128,896]{1,0:T(8,128)(2,1)S(1)} %multiply_convert_fusion.2.x), custom_call_target="tpu_custom_call" | custom-call | tf_op jit(solution)/shard_map/pallas_call | solution.py:158
  353.3 15.4 %shard_map.164 = f32[128,896]{1,0:T(8,128)S(1)} custom-call(bf16[8,128,896]{2,1,0:T(8,128)(2,1)S(1)} %bitcast.235), custom_call_target="tpu_custom_call" | custom-call | tf_op jit(solution)/shard_map/pallas_call | solution.py:158
  372.4 15.4 %shard_map.167 = f32[128,896]{1,0:T(8,128)S(1)} custom-call(bf16[8,128,896]{2,1,0:T(8,128)(2,1)S(1)} %bitcast.233), custom_call_target="tpu_custom_call" | custom-call | tf_op jit(solution)/shard_map/pallas_call | solution.py:158
  390.2 7.6 shard_map.168
  402.4 7.8 shard_map.169
  410.2 5.4 shard_map.170
  427.1 7.9 shard_map.171
  435.9 14.3 %shard_map.172 = bf16[8,128,896]{2,1,0:T(8,128)(2,1)S(1)} custom-call(bf16[128,896]{1,0:T(8,128)(2,1)S(1)} %get-tuple-element.84.x), custom_call_target="tpu_custom_call" | custom-call | tf_op jit(solution)/shard_map/pallas_call | solution.py:158
  458.6 15.7 %shard_map.173 = f32[128,896]{1,0:T(8,128)S(1)} custom-call(bf16[8,128,896]{2,1,0:T(8,128)(2,1)S(1)} %bitcast.234), custom_call_target="tpu_custom_call" | custom-call | tf_op jit(solution)/shard_map/pallas_call | solution.py:158
  475.5 7.4 shard_map.174
  493.7 7.6 shard_map.175
  501.3 5.4 shard_map.176
  518.1 10.1 %collective-permute-done.22 = bf16[1,608,224]{1,2,0:T(8,128)(2,1)S(1)} collective-permute-done((bf16[1,608,224]{1,2,0:T(8,128)(2,1)S(1)}, bf16[1,608,224]{1,2,0:T(8,128)(2,1)S(1)}, u32[]{:S(2)}, u32[]{:S(2)}) %collective-permute-start.22) | collective-permute-done | bytes 272416 | tf_op jit(solution)/shard_map/ppermute | solution.py:205
  528.3 5.4 collective-permute-done.23
  543.6 7.9 collective-permute-done.19
  551.6 5.0 collective-permute-done.20
  596.3 8.0 shard_map.177
  604.9 40.2 %psum.7 = f32[2,2944]{1,0:T(2,128)S(1)} all-reduce(f32[2,2944]{1,0:T(2,128)S(1)} %pad_maximum_fusion.3), channel_id=1, replica_groups=mesh['dp'=4,'grp'=2,'wid'=4] {'dp','grp','wid'}, use_global_device_ids=true, to_apply=%region_18.19 | all-reduce | flops 5888 | bytes 47104 | tf_op jit(solution)/shard_map/psum | solution.py:435
  645.5 10.4 %shard_map.165 = bf16[8,128,224]{2,1,0:T(8,128)(2,1)S(1)} custom-call(bf16[8,128,224]{2,1,0:T(8,128)(2,1)S(1)} %bitcast.215), custom_call_target="tpu_custom_call" | custom-call | tf_op jit(solution)/shard_map/pallas_call | solution.py:158
  657.8 9.1 %shard_map.178 = bf16[8,128,224]{2,1,0:T(8,128)(2,1)S(1)} custom-call(bf16[8,128,224]{2,1,0:T(8,128)(2,1)S(1)} %bitcast.217), custom_call_target="tpu_custom_call" | custom-call | tf_op jit(solution)/shard_map/pallas_call | solution.py:158
  674.4 29.8 %reduce-scatter.27.cloned.1.call-done = bf16[608,224]{1,0:T(8,128)(2,1)} async-done(((bf16[2432,224]{1,0:T(8,128)(2,1)}), bf16[608,224]{1,0:T(8,128)(2,1)}) %reduce-scatter.27.cloned.1.call-update) | async-done | bytes 272400
  705.3 30.1 %reduce-scatter.25.cloned.1.call-done = bf16[608,224]{1,0:T(8,128)(2,1)} async-done(((bf16[2432,224]{1,0:T(8,128)(2,1)}), bf16[608,224]{1,0:T(8,128)(2,1)}) %reduce-scatter.25.cloned.1.call-update) | async-done | bytes 272400
  737.7 45.9 %reduce-scatter.23.cloned.1.call-done = bf16[224,1216]{1,0:T(8,128)(2,1)} async-done(((bf16[896,1216]{1,0:T(8,128)(2,1)}), bf16[224,1216]{1,0:T(8,128)(2,1)}) %reduce-scatter.23.cloned.1.call-update) | async-done | bytes 544784 | tf_op jit(solution)/shard_map/reduce_scatter | solution.py:401
  784.6 47.9 %reduce-scatter.21.cloned.1.call-done = bf16[224,1216]{1,0:T(8,128)(2,1)} async-done(((bf16[896,1216]{1,0:T(8,128)(2,1)}), bf16[224,1216]{1,0:T(8,128)(2,1)}) %reduce-scatter.21.cloned.1.call-update) | async-done | bytes 544784 | tf_op jit(solution)/shard_map/reduce_scatter | solution.py:401
  839.0 6.0 collective-permute-done.16
  (440 shorter events, 220.7 us)
Async XLA Ops:
  7.2 662.4 %reduce-scatter.19.cloned.1.call-start = ((), (), s32[]{:S(2)}) async-start(), calls=%async_computation.9 | async-start | bytes 974848 | tf_op jit(solution)/shard_map/reduce_scatter | solution.py:424
  11.4 225.9 %collective-permute-start.11 = (bf16[1,608,224]{1,2,0:T(8,128)(2,1)}, bf16[1,608,224]{1,2,0:T(8,128)(2,1)}, u32[]{:S(2)}, u32[]{:S(2)}) collective-permute-start(bf16[1,608,224]{1,2,0:T(8,128)(2,1)} %get-tuple-element.123), channel_id=1, source_target_pairs={{0,3},{1,2},{2,1},{3,0},{4,7},{5,6},{6,5},{7,4},{8,11},{9,10},{10,... | collective-permute-start | bytes 817160 | tf_op jit(solution)/shard_map/ppermute | solution.py:205
  13.8 221.5 %collective-permute-start.10 = (bf16[1,608,224]{1,2,0:T(8,128)(2,1)}, bf16[1,608,224]{1,2,0:T(8,128)(2,1)}, u32[]{:S(2)}, u32[]{:S(2)}) collective-permute-start(bf16[1,608,224]{1,2,0:T(8,128)(2,1)} %get-tuple-element.124), channel_id=1, source_target_pairs={{0,2},{1,3},{2,0},{3,1},{4,6},{5,7},{6,4},{7,5},{8,10},{9,11},{10,... | collective-permute-start | bytes 817160 | tf_op jit(solution)/shard_map/ppermute | solution.py:205
  14.4 217.6 %collective-permute-start.9 = (bf16[1,608,224]{1,2,0:T(8,128)(2,1)}, bf16[1,608,224]{1,2,0:T(8,128)(2,1)}, u32[]{:S(2)}, u32[]{:S(2)}) collective-permute-start(bf16[1,608,224]{1,2,0:T(8,128)(2,1)} %get-tuple-element.125), channel_id=1, source_target_pairs={{0,1},{1,0},{2,3},{3,2},{4,5},{5,4},{6,7},{7,6},{8,9},{9,8},{10,11... | collective-permute-start | bytes 817160 | tf_op jit(solution)/shard_map/ppermute | solution.py:205
  17.9 223.9 %collective-permute-start.5 = (bf16[1,608,224]{1,2,0:T(8,128)(2,1)}, bf16[1,608,224]{1,2,0:T(8,128)(2,1)}, u32[]{:S(2)}, u32[]{:S(2)}) collective-permute-start(bf16[1,608,224]{1,2,0:T(8,128)(2,1)} %get-tuple-element.126), channel_id=1, source_target_pairs={{0,3},{1,2},{2,1},{3,0},{4,7},{5,6},{6,5},{7,4},{8,11},{9,10},{10,... | collective-permute-start | bytes 817160 | tf_op jit(solution)/shard_map/ppermute | solution.py:205
  19.3 214.7 %collective-permute-start.3 = (bf16[1,608,224]{1,2,0:T(8,128)(2,1)}, bf16[1,608,224]{1,2,0:T(8,128)(2,1)}, u32[]{:S(2)}, u32[]{:S(2)}) collective-permute-start(bf16[1,608,224]{1,2,0:T(8,128)(2,1)} %get-tuple-element.128), channel_id=1, source_target_pairs={{0,1},{1,0},{2,3},{3,2},{4,5},{5,4},{6,7},{7,6},{8,9},{9,8},{10,11... | collective-permute-start | bytes 817160 | tf_op jit(solution)/shard_map/ppermute | solution.py:205
  19.7 289.0 %copy-start.68 = (pred[576]{0:T(1024)(128)(4,1)}, pred[576]{0:T(1024)(128)(4,1)S(1)}, u32[]{:S(2)}) copy-start(pred[576]{0:T(1024)(128)(4,1)S(1)} %fusion.50) | copy-start | bytes 1732
  20.1 30.9 %copy-start.58 = (bf16[1,1024,224]{1,2,0:T(8,128)(2,1)S(1)}, bf16[1,1024,224]{1,2,0:T(8,128)(2,1)}, u32[]{:S(2)}) copy-start(bf16[1,1024,224]{1,2,0:T(8,128)(2,1)} %param.17) | copy-start | bytes 1376260
  20.1 30.9 %copy-start.59 = (bf16[1,1024,224]{1,2,0:T(8,128)(2,1)S(1)}, bf16[1,1024,224]{1,2,0:T(8,128)(2,1)}, u32[]{:S(2)}) copy-start(bf16[1,1024,224]{1,2,0:T(8,128)(2,1)} %param.9) | copy-start | bytes 1376260
  51.0 336.8 %copy-start.63 = (f32[896]{0:T(1024)}, f32[896]{0:T(1024)S(1)}, u32[]{:S(2)}) copy-start(f32[896]{0:T(1024)S(1)} %get-tuple-element.72) | copy-start | bytes 10756
  65.2 19.7 %copy-start.75 = (f32[128]{0:T(128)}, f32[128]{0:T(128)S(1)}, u32[]{:S(2)}) copy-start(f32[128]{0:T(128)S(1)} %get-tuple-element.160) | copy-start | bytes 1540
  90.6 218.1 %copy-start.17 = (f32[256,576]{1,0:T(8,128)}, f32[256,576]{1,0:T(8,128)S(1)}, u32[]{:S(2)}) copy-start(f32[256,576]{1,0:T(8,128)S(1)} %concatenate.56) | copy-start | bytes 1769476
  93.5 39.5 %copy-start.8 = (bf16[256,448]{1,0:T(8,128)(2,1)}, bf16[256,448]{1,0:T(8,128)(2,1)S(1)}, u32[]{:S(2)}) copy-start(bf16[256,448]{1,0:T(8,128)(2,1)S(1)} %slice.204.q) | copy-start | bytes 688132
  201.1 30.9 %copy-start.61 = (bf16[1,608,224]{1,2,0:T(8,128)(2,1)S(1)}, bf16[1,608,224]{1,2,0:T(8,128)(2,1)}, u32[]{:S(2)}) copy-start(bf16[1,608,224]{1,2,0:T(8,128)(2,1)} %get-tuple-element.127) | copy-start | bytes 817156
  201.1 32.9 %copy-start.56 = (bf16[1,2,224,608]{3,2,0,1:T(8,128)(2,1)S(1)}, bf16[1,2,224,608]{3,2,0,1:T(8,128)(2,1)}, u32[]{:S(2)}) copy-start(bf16[1,2,224,608]{3,2,0,1:T(8,128)(2,1)} %get-tuple-element.112) | copy-start | bytes 1634308
  216.9 50.1 %copy-start = (bf16[8,128,896]{2,1,0:T(8,128)(2,1)}, bf16[8,128,896]{2,1,0:T(8,128)(2,1)S(1)}, u32[]{:S(2)}) copy-start(bf16[8,128,896]{2,1,0:T(8,128)(2,1)S(1)} %shard_map.157) | copy-start | bytes 5505028
  216.9 17.3 %copy-start.40 = (bf16[4,608,224]{1,2,0:T(8,128)(2,1)S(1)}, bf16[4,608,224]{1,2,0:T(8,128)(2,1)}, u32[]{:S(2)}) copy-start(bf16[4,608,224]{1,2,0:T(8,128)(2,1)} %copy-done.39) | copy-start | bytes 3268612
  232.0 116.2 %copy-start.2 = (bf16[8,128,896]{2,1,0:T(8,128)(2,1)}, bf16[8,128,896]{2,1,0:T(8,128)(2,1)S(1)}, u32[]{:S(2)}) copy-start(bf16[8,128,896]{2,1,0:T(8,128)(2,1)S(1)} %shard_map.166) | copy-start | bytes 5505028
  232.0 9.7 %collective-permute-start.4 = (bf16[1,608,224]{1,2,0:T(8,128)(2,1)S(1)}, bf16[1,608,224]{1,2,0:T(8,128)(2,1)S(1)}, u32[]{:S(2)}, u32[]{:S(2)}) collective-permute-start(bf16[1,608,224]{1,2,0:T(8,128)(2,1)S(1)} %copy-done.61), channel_id=1, source_target_pairs={{0,2},{1,3},{2,0},{3,1},{4,6},{5,7},{6,4},{7,5},{8,10},{9,11},{10,... | collective-permute-start | bytes 817160 | tf_op jit(solution)/shard_map/ppermute | solution.py:205
  234.0 9.8 %collective-permute-start = (bf16[1,2,224,608]{3,2,0,1:T(8,128)(2,1)S(1)}, bf16[1,2,224,608]{3,2,0,1:T(8,128)(2,1)S(1)}, u32[]{:S(2)}, u32[]{:S(2)}) collective-permute-start(bf16[1,2,224,608]{3,2,0,1:T(8,128)(2,1)S(1)} %copy-done.56), channel_id=1, source_target_pairs={{0,1},{1,0},{2,3},{3,2},{4,5},{5,4},{6,7},{7,6},{8,9},{9,8},{10,11... | collective-permute-start | bytes 1634312 | tf_op jit(solution)/shard_map/ppermute | solution.py:205
  235.3 18.8 %collective-permute-start.1 = (bf16[1,2,224,608]{3,2,0,1:T(8,128)(2,1)}, bf16[1,2,224,608]{3,2,0,1:T(8,128)(2,1)S(1)}, u32[]{:S(2)}, u32[]{:S(2)}) collective-permute-start(bf16[1,2,224,608]{3,2,0,1:T(8,128)(2,1)} %get-tuple-element.111), channel_id=1, source_target_pairs={{0,2},{1,3},{2,0},{3,1},{4,6},{5,7},{6,4},{7,5},{8,10},{9,11},{10,... | collective-permute-start | bytes 1634312 | tf_op jit(solution)/shard_map/ppermute | solution.py:205
  237.4 27.8 %collective-permute-start.2 = (bf16[1,2,224,608]{3,2,0,1:T(8,128)(2,1)S(1)}, bf16[1,2,224,608]{3,2,0,1:T(8,128)(2,1)S(1)}, u32[]{:S(2)}, u32[]{:S(2)}) collective-permute-start(bf16[1,2,224,608]{3,2,0,1:T(8,128)(2,1)S(1)} %copy-done.55), channel_id=1, source_target_pairs={{0,3},{1,2},{2,1},{3,0},{4,7},{5,6},{6,5},{7,4},{8,11},{9,10},{10,... | collective-permute-start | bytes 1634312 | tf_op jit(solution)/shard_map/ppermute | solution.py:205
  241.7 69.7 %collective-permute-start.8 = (bf16[1,2,224,608]{3,2,0,1:T(8,128)(2,1)}, bf16[1,2,224,608]{3,2,0,1:T(8,128)(2,1)S(1)}, u32[]{:S(2)}, u32[]{:S(2)}) collective-permute-start(bf16[1,2,224,608]{3,2,0,1:T(8,128)(2,1)} %get-tuple-element.103), channel_id=1, source_target_pairs={{0,3},{1,2},{2,1},{3,0},{4,7},{5,6},{6,5},{7,4},{8,11},{9,10},{10,... | collective-permute-start | bytes 1634312 | tf_op jit(solution)/shard_map/ppermute | solution.py:205
  241.8 69.6 %collective-permute-start.7 = (bf16[1,2,224,608]{3,2,0,1:T(8,128)(2,1)}, bf16[1,2,224,608]{3,2,0,1:T(8,128)(2,1)S(1)}, u32[]{:S(2)}, u32[]{:S(2)}) collective-permute-start(bf16[1,2,224,608]{3,2,0,1:T(8,128)(2,1)} %get-tuple-element.104), channel_id=1, source_target_pairs={{0,2},{1,3},{2,0},{3,1},{4,6},{5,7},{6,4},{7,5},{8,10},{9,11},{10,... | collective-permute-start | bytes 1634312 | tf_op jit(solution)/shard_map/ppermute | solution.py:205
  243.8 26.1 %copy-start.41 = (bf16[4,608,224]{1,2,0:T(8,128)(2,1)}, bf16[4,608,224]{1,2,0:T(8,128)(2,1)S(1)}, u32[]{:S(2)}) copy-start(bf16[4,608,224]{1,2,0:T(8,128)(2,1)S(1)} %constant_dynamic-update-slice_fusion.18) | copy-start | bytes 3268612
  243.8 66.2 %collective-permute-start.6 = (bf16[1,2,224,608]{3,2,0,1:T(8,128)(2,1)}, bf16[1,2,224,608]{3,2,0,1:T(8,128)(2,1)S(1)}, u32[]{:S(2)}, u32[]{:S(2)}) collective-permute-start(bf16[1,2,224,608]{3,2,0,1:T(8,128)(2,1)} %get-tuple-element.105), channel_id=1, source_target_pairs={{0,1},{1,0},{2,3},{3,2},{4,5},{5,4},{6,7},{7,6},{8,9},{9,8},{10,11... | collective-permute-start | bytes 1634312 | tf_op jit(solution)/shard_map/ppermute | solution.py:205
  271.7 28.8 %copy-start.26 = (f32[128,896]{1,0:T(8,128)S(1)}, f32[128,896]{1,0:T(8,128)}, u32[]{:S(2)}) copy-start(f32[128,896]{1,0:T(8,128)} %get-tuple-element.93) | copy-start | bytes 1376260
  300.6 29.8 %copy-start.28 = (f32[128,896]{1,0:T(8,128)}, f32[128,896]{1,0:T(8,128)S(1)}, u32[]{:S(2)}) copy-start(f32[128,896]{1,0:T(8,128)S(1)} %get-tuple-element.91) | copy-start | bytes 1376260
  351.5 19.1 %copy-start.79 = (bf16[1024,608]{0,1:T(8,128)(2,1)}, bf16[1024,608]{0,1:T(8,128)(2,1)S(1)}, u32[]{:S(2)}) copy-start(bf16[1024,608]{0,1:T(8,128)(2,1)S(1)} %get-tuple-element.96) | copy-start | bytes 3735556
  423.6 245.9 %reduce-scatter.17.cloned.1.call-start = ((), (), s32[]{:S(2)}) async-start(), calls=%async_computation.8 | async-start | bytes 974848 | tf_op jit(solution)/shard_map/reduce_scatter | solution.py:424
  490.0 181.1 %reduce-scatter.31.cloned.1.call-start = ((), (), s32[]{:S(2)}) async-start(), calls=%async_computation.15 | async-start | bytes 1218560
  491.7 181.1 %reduce-scatter.29.cloned.1.call-start = ((), (), s32[]{:S(2)}) async-start(), calls=%async_computation.14 | async-start | bytes 1218560
  510.1 194.1 %reduce-scatter.27.cloned.1.call-start = ((), (), s32[]{:S(2)}) async-start(), calls=%async_computation.13 | async-start | bytes 1556480
  516.1 1.9 collective-permute-start.21
  516.5 11.7 %collective-permute-start.22 = (bf16[1,608,224]{1,2,0:T(8,128)(2,1)S(1)}, bf16[1,608,224]{1,2,0:T(8,128)(2,1)S(1)}, u32[]{:S(2)}, u32[]{:S(2)}) collective-permute-start(bf16[1,608,224]{1,2,0:T(8,128)(2,1)S(1)} %get-tuple-element.121), channel_id=1, source_target_pairs={{0,2},{1,3},{2,0},{3,1},{4,6},{5,7},{6,4},{7,5},{8,10},{9,11},{10,... | collective-permute-start | bytes 817160 | tf_op jit(solution)/shard_map/ppermute | solution.py:205
  517.5 16.2 %collective-permute-start.23 = (bf16[1,608,224]{1,2,0:T(8,128)(2,1)S(1)}, bf16[1,608,224]{1,2,0:T(8,128)(2,1)S(1)}, u32[]{:S(2)}, u32[]{:S(2)}) collective-permute-start(bf16[1,608,224]{1,2,0:T(8,128)(2,1)S(1)} %get-tuple-element.120), channel_id=1, source_target_pairs={{0,3},{1,2},{2,1},{3,0},{4,7},{5,6},{6,5},{7,4},{8,11},{9,10},{10,... | collective-permute-start | bytes 817160 | tf_op jit(solution)/shard_map/ppermute | solution.py:205
  535.2 200.2 %reduce-scatter.25.cloned.1.call-start = ((), (), s32[]{:S(2)}) async-start(), calls=%async_computation.12 | async-start | bytes 1556480
  541.6 1.9 collective-permute-start.18
  541.9 9.7 %collective-permute-start.19 = (bf16[1,608,224]{1,2,0:T(8,128)(2,1)S(1)}, bf16[1,608,224]{1,2,0:T(8,128)(2,1)S(1)}, u32[]{:S(2)}, u32[]{:S(2)}) collective-permute-start(bf16[1,608,224]{1,2,0:T(8,128)(2,1)S(1)} %get-tuple-element.118), channel_id=1, source_target_pairs={{0,2},{1,3},{2,0},{3,1},{4,6},{5,7},{6,4},{7,5},{8,10},{9,11},{10,... | collective-permute-start | bytes 817160 | tf_op jit(solution)/shard_map/ppermute | solution.py:205
  542.7 13.8 %collective-permute-start.20 = (bf16[1,608,224]{1,2,0:T(8,128)(2,1)S(1)}, bf16[1,608,224]{1,2,0:T(8,128)(2,1)S(1)}, u32[]{:S(2)}, u32[]{:S(2)}) collective-permute-start(bf16[1,608,224]{1,2,0:T(8,128)(2,1)S(1)} %get-tuple-element.117), channel_id=1, source_target_pairs={{0,3},{1,2},{2,1},{3,0},{4,7},{5,6},{6,5},{7,4},{8,11},{9,10},{10,... | collective-permute-start | bytes 817160 | tf_op jit(solution)/shard_map/ppermute | solution.py:205
  558.1 225.4 %reduce-scatter.23.cloned.1.call-start = ((), (), s32[]{:S(2)}) async-start(), calls=%async_computation.11 | async-start | bytes 2867200 | tf_op jit(solution)/shard_map/reduce_scatter | solution.py:401
  575.7 256.8 %reduce-scatter.21.cloned.1.call-start = ((), (), s32[]{:S(2)}) async-start(), calls=%async_computation.10 | async-start | bytes 2867200 | tf_op jit(solution)/shard_map/reduce_scatter | solution.py:401
  784.5 49.1 %collective-permute-start.15 = (bf16[1,56,1216]{2,1,0:T(8,128)(2,1)S(1)}, bf16[1,56,1216]{2,1,0:T(8,128)(2,1)S(1)}, u32[]{:S(2)}, u32[]{:S(2)}) collective-permute-start(bf16[1,56,1216]{2,1,0:T(8,128)(2,1)S(1)} %constant_dynamic-slice_fusion.4), channel_id=1, source_target_pairs={{0,1},{1,0},{2,3},{3,2},{4,5},{5,4},{6,7},{7,6},{8,9},{9,8},{10,11... | collective-permute-start | bytes 408584 | tf_op jit(solution)/shard_map/ppermute | solution.py:205
  833.5 3.9 collective-permute-start.12
  835.3 10.4 %collective-permute-start.17 = (bf16[1,56,1216]{2,1,0:T(8,128)(2,1)S(1)}, bf16[1,56,1216]{2,1,0:T(8,128)(2,1)S(1)}, u32[]{:S(2)}, u32[]{:S(2)}) collective-permute-start(bf16[1,56,1216]{2,1,0:T(8,128)(2,1)S(1)} %get-tuple-element.146), channel_id=1, source_target_pairs={{0,3},{1,2},{2,1},{3,0},{4,7},{5,6},{6,5},{7,4},{8,11},{9,10},{10,... | collective-permute-start | bytes 408584 | tf_op jit(solution)/shard_map/ppermute | solution.py:205
  836.8 8.2 collective-permute-start.16
  837.4 13.1 %collective-permute-start.14 = (bf16[1,56,1216]{2,1,0:T(8,128)(2,1)S(1)}, bf16[1,56,1216]{2,1,0:T(8,128)(2,1)S(1)}, u32[]{:S(2)}, u32[]{:S(2)}) collective-permute-start(bf16[1,56,1216]{2,1,0:T(8,128)(2,1)S(1)} %get-tuple-element.143), channel_id=1, source_target_pairs={{0,3},{1,2},{2,1},{3,0},{4,7},{5,6},{6,5},{7,4},{8,11},{9,10},{10,... | collective-permute-start | bytes 408584 | tf_op jit(solution)/shard_map/ppermute | solution.py:205
  838.3 12.2 %collective-permute-start.13 = (bf16[1,56,1216]{2,1,0:T(8,128)(2,1)S(1)}, bf16[1,56,1216]{2,1,0:T(8,128)(2,1)S(1)}, u32[]{:S(2)}, u32[]{:S(2)}) collective-permute-start(bf16[1,56,1216]{2,1,0:T(8,128)(2,1)S(1)} %get-tuple-element.144), channel_id=1, source_target_pairs={{0,2},{1,3},{2,0},{3,1},{4,6},{5,7},{6,4},{7,5},{8,10},{9,11},{10,... | collective-permute-start | bytes 408584 | tf_op jit(solution)/shard_map/ppermute | solution.py:205
  (73 other events, 384.6 us)
Sparse Core Ops, SparseCore 0:
  423.7 57.1 reduce-scatter.18
  490.1 59.5 reduce-scatter.16
  554.0 56.9 reduce-scatter.30
  614.6 58.0 reduce-scatter.28
  674.9 29.1 reduce-scatter.26
  706.5 28.9 reduce-scatter.24
  737.8 45.7 reduce-scatter.22
  786.0 46.4 reduce-scatter.20
